TPU v7x, 32 devices: a whole 2x2x4 slice. The times are simulated.
32 devices in a mesh: dp: 8 (over y, x, core), mp: 4 (over z).
Axes of the slice: x: 2, y: 2, z: 4, core: 2. Of those that a mesh axis runs over, the one named last changes fastest.
Arguments:
- byte_ids: int32 [16384], P(('dp', 'mp')), may hold values from 0 to 255
- embed_table: bfloat16 [256, 512], replicated, may hold values from -6 to 6
- boundary_labels: int32 [16384], P('dp'), may hold values 0 or 1
- out_cotangent: bfloat16 [16384, 512], P(('dp', 'mp')), may hold values from -6 to 6
- norm_one_gain: bfloat16 [512], replicated, may hold values from 0.5 to 1.5
- norm_one_bias: bfloat16 [512], replicated, may hold values from -2 to 2
- w_query: bfloat16 [512, 512], P(None, 'mp'), may hold values from -0.25 to 0.25
- w_key: bfloat16 [512, 512], P(None, 'mp'), may hold values from -0.25 to 0.25
- w_value: bfloat16 [512, 512], P(None, 'mp'), may hold values from -0.25 to 0.25
- w_position: bfloat16 [512, 512], P(None, 'mp'), may hold values from -0.25 to 0.25
- content_bias: bfloat16 [8, 64], P('mp'), may hold values from -3 to 3
- position_bias: bfloat16 [8, 64], P('mp'), may hold values from -3 to 3
- w_out: bfloat16 [512, 512], P('mp'), may hold values from -0.75 to 0.75
- norm_two_gain: bfloat16 [512], replicated, may hold values from 0.5 to 1.5
- norm_two_bias: bfloat16 [512], replicated, may hold values from -2 to 2
- w_up: bfloat16 [512, 2048], P(None, 'mp'), may hold values from -0.25 to 0.25
- up_bias: bfloat16 [2048], P('mp'), may hold values from -2 to 2
- w_down: bfloat16 [2048, 512], P('mp'), may hold values from -0.125 to 0.125
- down_bias: bfloat16 [512], replicated, may hold values from -2 to 2
- w_pred: bfloat16 [512, 2048], P(None, 'mp'), may hold values from -0.25 to 0.25
- pred_bias: bfloat16 [2048], P('mp'), may hold values from -2 to 2
- w_logit: bfloat16 [2048], P('mp'), may hold values from -0.5 to 0.5
- logit_bias: bfloat16 [1], replicated, may hold values from -1 to 1
Outputs:
- block_out: bfloat16 [16384, 512], P(('dp', 'mp'))
- loss_value: float32 [1], replicated
- grad_input: bfloat16 [16384, 512], P(('dp', 'mp'))
- grad_embed: float32 [256, 512], replicated
- grad_norm_one_gain: float32 [512], replicated
- grad_norm_one_bias: float32 [512], replicated
- grad_w_query: float32 [512, 512], P(None, 'mp')
- grad_w_key: float32 [512, 512], P(None, 'mp')
- grad_w_value: float32 [512, 512], P(None, 'mp')
- grad_w_position: float32 [512, 512], P(None, 'mp')
- grad_content_bias: float32 [8, 64], P('mp')
- grad_position_bias: float32 [8, 64], P('mp')
- grad_w_out: float32 [512, 512], P('mp')
- grad_norm_two_gain: float32 [512], replicated
- grad_norm_two_bias: float32 [512], replicated
- grad_w_up: float32 [512, 2048], P(None, 'mp')
- grad_up_bias: float32 [2048], P('mp')
- grad_w_down: float32 [2048, 512], P('mp')
- grad_down_bias: float32 [512], replicated
- grad_w_pred: float32 [512, 2048], P(None, 'mp')
- grad_pred_bias: float32 [2048], P('mp')
- grad_w_logit: float32 [2048], P('mp')
- grad_logit_bias: float32 [1], replicated
All inputs are finite; a program needn't handle non-finite values. No bound on the sum of `boundary_labels` on one device may be relied on, other than what follows from the above.
Results may differ from a plain program's by a relative error of at most 0.025.
Values may be sent and summed in bfloat16 or wider, within the bound.
No kernel may reach another device: no remote copies, remote signals or barrier semaphores. Data moves between devices by JAX's collectives and lax.ppermute only.
A program may use at most 192 MiB of HBM per device.

v0:
```python
import math

import jax
import jax.numpy as jnp
from jax import lax
from jax.sharding import PartitionSpec as P

LEN = 2048


norm_eps = 1e-05
half_root = 1.0 / math.sqrt(2.0)
density_scale = 1.0 / math.sqrt(2.0 * math.pi)


def layer_stats(values):
    centered = values - jnp.mean(values, axis=-1, keepdims=True)
    inverse = lax.rsqrt(jnp.mean(centered * centered, axis=-1, keepdims=True) + norm_eps)
    return (centered * inverse, inverse)


def norm_back(grad_normed, normed, inverse, gain_row):
    scaled = grad_normed * gain_row
    first_mean = jnp.mean(scaled, axis=-1, keepdims=True)
    second_mean = jnp.mean(scaled * normed, axis=-1, keepdims=True)
    return inverse * (scaled - first_mean - normed * second_mean)


def gelu_slope(values):
    return (
        0.5 * (1.0 + jax.scipy.special.erf(values * half_root))
        + values * jnp.exp(-0.5 * values * values) * density_scale
    )


def rotation_tables(length, model_width):
    frequency = jnp.exp(
        jnp.arange(model_width // 2, dtype=jnp.float32) * (-2.0 * math.log(10000.0) / model_width)
    )
    angles = jnp.arange(length, dtype=jnp.float32)[:, None] * frequency[None, :]
    return (jnp.sin(angles), jnp.cos(angles))


def own_slice(values, first_row, own_rows):
    return lax.dynamic_slice_in_dim(values, first_row, own_rows, 0)


def add_rows(values, extra, first_row):
    current = lax.dynamic_slice_in_dim(values, first_row, extra.shape[0], 0)
    return lax.dynamic_update_slice_in_dim(values, current + extra, first_row, 0)


def per_device(
    byte_ids,
    embed_table,
    boundary_labels,
    out_cotangent,
    norm_one_gain,
    norm_one_bias,
    w_query,
    w_key,
    w_value,
    w_position,
    content_bias,
    position_bias,
    w_out,
    norm_two_gain,
    norm_two_bias,
    w_up,
    up_bias,
    w_down,
    down_bias,
    w_pred,
    pred_bias,
    w_logit,
    logit_bias,
):
    own_rows = byte_ids.shape[0]
    all_rows = boundary_labels.shape[0]
    model_width = embed_table.shape[1]
    half_width = model_width // 2
    head_count = content_bias.shape[0]
    head_size = content_bias.shape[1]
    local_width = head_count * head_size
    seq_count = all_rows // LEN
    block_rows = min(512, LEN)
    first_row = lax.axis_index("mp") * own_rows
    score_scale = 1.0 / math.sqrt(head_size)
    gain_one = norm_one_gain.astype(jnp.float32)
    gain_two = norm_two_gain.astype(jnp.float32)
    bias_two = norm_two_bias.astype(jnp.float32)
    vocab_ids = jnp.arange(embed_table.shape[0], dtype=jnp.int32)
    one_hot = (byte_ids[:, None] == vocab_ids[None, :]).astype(jnp.bfloat16)
    inputs = jnp.dot(one_hot, embed_table, preferred_element_type=jnp.float32)
    normed_one, inverse_one = layer_stats(inputs)
    norm_in = (normed_one * gain_one + norm_one_bias.astype(jnp.float32)).astype(jnp.bfloat16)
    norm_all = lax.all_gather(norm_in, "mp", axis=0, tiled=True)
    w_joint = jnp.concatenate([w_query, w_key, w_value], axis=1)
    joint_proj = jnp.dot(norm_all, w_joint, preferred_element_type=jnp.float32)
    query_raw = joint_proj[:, :local_width]
    key_rows = joint_proj[:, local_width : 2 * local_width].astype(jnp.bfloat16)
    value_rows = joint_proj[:, 2 * local_width :].astype(jnp.bfloat16)
    query_content = (query_raw + content_bias.reshape(local_width).astype(jnp.float32)).astype(
        jnp.bfloat16
    )
    query_shift = (query_raw + position_bias.reshape(local_width).astype(jnp.float32)).astype(
        jnp.bfloat16
    )
    shift_heads = query_shift.reshape(all_rows, head_count, head_size)
    pos_weight = w_position.reshape(model_width, head_count, head_size)
    coeffs = jnp.einsum("she,mhe->shm", shift_heads, pos_weight, preferred_element_type=jnp.float32)
    sines, cosines = rotation_tables(LEN, model_width)
    sine_rows = jnp.tile(sines, (seq_count, 1))[:, None, :]
    cosine_rows = jnp.tile(cosines, (seq_count, 1))[:, None, :]
    coeff_sin = coeffs[:, :, :half_width]
    coeff_cos = coeffs[:, :, half_width:]
    pos_query = jnp.concatenate(
        [
            coeff_sin * sine_rows + coeff_cos * cosine_rows,
            coeff_cos * sine_rows - coeff_sin * cosine_rows,
        ],
        axis=-1,
    ).astype(jnp.bfloat16)
    key_feature = jnp.concatenate([cosines, sines], axis=-1).astype(jnp.bfloat16)
    content_seq = query_content.reshape(seq_count, LEN, head_count, head_size)
    key_seq = key_rows.reshape(seq_count, LEN, head_count, head_size)
    value_seq = value_rows.reshape(seq_count, LEN, head_count, head_size)
    posq_seq = pos_query.reshape(seq_count, LEN, head_count, model_width)

    def block_scores(block_index):
        row_low = block_index * block_rows
        row_high = row_low + block_rows
        content_part = jnp.einsum(
            "sqhe,skhe->shqk",
            content_seq[:, row_low:row_high],
            key_seq[:, :row_high],
            preferred_element_type=jnp.float32,
        )
        relative_part = jnp.einsum(
            "sqhm,km->shqk",
            posq_seq[:, row_low:row_high],
            key_feature[:row_high],
            preferred_element_type=jnp.float32,
        )
        scores = score_scale * (content_part + relative_part)
        query_places = row_low + jnp.arange(block_rows)
        allowed = query_places[:, None] >= jnp.arange(row_high)[None, :]
        return jnp.where(allowed, scores, -1000000000.0)

    attended_blocks = []
    lse_blocks = []
    for block_index in range(LEN // block_rows):
        row_high = (block_index + 1) * block_rows
        scores = block_scores(block_index)
        row_top = jnp.max(scores, axis=-1, keepdims=True)
        expon = jnp.exp(scores - row_top)
        row_total = jnp.sum(expon, axis=-1, keepdims=True)
        probs_low = (expon / row_total).astype(jnp.bfloat16)
        lse_blocks.append(row_top + jnp.log(row_total))
        attended_blocks.append(
            jnp.einsum(
                "shqk,skhe->sqhe",
                probs_low,
                value_seq[:, :row_high],
                preferred_element_type=jnp.float32,
            ).astype(jnp.bfloat16)
        )
    attended_seq = jnp.concatenate(attended_blocks, axis=1)
    attended = attended_seq.reshape(all_rows, local_width)
    attn_part = jnp.dot(attended, w_out, preferred_element_type=jnp.float32)
    attn_part = add_rows(attn_part, inputs, first_row)
    middle = lax.psum(attn_part.astype(jnp.bfloat16), "mp").astype(jnp.float32)
    normed_two, inverse_two = layer_stats(middle)
    norm_mid = (normed_two * gain_two + bias_two).astype(jnp.bfloat16)
    normed_two_own = own_slice(normed_two, first_row, own_rows)
    up_pre = jnp.dot(norm_mid, w_up, preferred_element_type=jnp.float32) + up_bias.astype(
        jnp.float32
    )
    hidden = jax.nn.gelu(up_pre, approximate=False).astype(jnp.bfloat16)
    down_shift = down_bias.astype(jnp.float32)
    ffn_part = jnp.dot(hidden, w_down, preferred_element_type=jnp.float32)
    out_full = (
        middle + lax.psum(ffn_part.astype(jnp.bfloat16), "mp").astype(jnp.float32) + down_shift
    )
    out_low = out_full.astype(jnp.bfloat16)
    out_low_own = own_slice(out_low, first_row, own_rows)
    pred_pre = jnp.dot(out_low, w_pred, preferred_element_type=jnp.float32) + pred_bias.astype(
        jnp.float32
    )
    pred_hidden = jax.nn.gelu(pred_pre, approximate=False).astype(jnp.bfloat16)
    logit_part = jnp.dot(pred_hidden, w_logit, preferred_element_type=jnp.float32)
    logits = lax.psum(logit_part, "mp") + logit_bias.astype(jnp.float32)[0]
    labels_float = boundary_labels.astype(jnp.float32)
    loss_part = jnp.sum(jax.nn.softplus(logits) - labels_float * logits).reshape(1)
    grad_logit = jax.nn.sigmoid(logits) - labels_float
    grad_logit_bias = jnp.sum(grad_logit).reshape(1)
    grad_logit_low = grad_logit.astype(jnp.bfloat16)
    grad_w_logit = jnp.dot(grad_logit_low, pred_hidden, preferred_element_type=jnp.float32)
    grad_pred_pre = (
        grad_logit_low.astype(jnp.float32)[:, None]
        * w_logit.astype(jnp.float32)[None, :]
        * gelu_slope(pred_pre)
    )
    grad_pred_bias = jnp.sum(grad_pred_pre, axis=0)
    grad_pred_low = grad_pred_pre.astype(jnp.bfloat16)
    grad_w_pred = jnp.einsum(
        "sd,sf->df", out_low, grad_pred_low, preferred_element_type=jnp.float32
    )
    pred_back = jnp.einsum("sf,df->sd", grad_pred_low, w_pred, preferred_element_type=jnp.float32)
    pred_back = add_rows(pred_back, out_cotangent.astype(jnp.float32), first_row)
    grad_out = lax.psum(pred_back.astype(jnp.bfloat16), "mp").astype(jnp.float32)
    grad_out_low = grad_out.astype(jnp.bfloat16)
    grad_out_own = own_slice(grad_out, first_row, own_rows)
    grad_down_bias = jnp.sum(grad_out_own, axis=0)
    grad_w_down = jnp.einsum("sf,sd->fd", hidden, grad_out_low, preferred_element_type=jnp.float32)
    grad_hidden = jnp.einsum("sd,fd->sf", grad_out_low, w_down, preferred_element_type=jnp.float32)
    grad_up_pre = grad_hidden * gelu_slope(up_pre)
    grad_up_bias = jnp.sum(grad_up_pre, axis=0)
    grad_up_low = grad_up_pre.astype(jnp.bfloat16)
    grad_w_up = jnp.einsum("sd,sf->df", norm_mid, grad_up_low, preferred_element_type=jnp.float32)
    grad_mid_part = jnp.einsum("sf,df->sd", grad_up_low, w_up, preferred_element_type=jnp.float32)
    grad_mid = lax.psum(grad_mid_part.astype(jnp.bfloat16), "mp").astype(jnp.float32)
    grad_resid = grad_out + norm_back(grad_mid, normed_two, inverse_two, gain_two)
    grad_attn_low = grad_resid.astype(jnp.bfloat16)
    grad_resid_own = own_slice(grad_resid, first_row, own_rows)
    grad_mid_own = own_slice(grad_mid, first_row, own_rows)
    grad_gain_two = jnp.sum(grad_mid_own * normed_two_own, axis=0)
    grad_bias_two = jnp.sum(grad_mid_own, axis=0)
    grad_w_out = jnp.einsum(
        "se,sd->ed", attended, grad_attn_low, preferred_element_type=jnp.float32
    )
    grad_attended = jnp.einsum(
        "sd,ed->se", grad_attn_low, w_out, preferred_element_type=jnp.float32
    ).astype(jnp.bfloat16)
    grad_att_seq = grad_attended.reshape(seq_count, LEN, head_count, head_size)
    grad_key_acc = jnp.zeros((seq_count, LEN, head_count, head_size), jnp.float32)
    grad_value_acc = jnp.zeros((seq_count, LEN, head_count, head_size), jnp.float32)
    content_grads = []
    posq_grads = []
    for block_index in range(LEN // block_rows):
        row_low = block_index * block_rows
        row_high = row_low + block_rows
        scores = block_scores(block_index)
        probs = jnp.exp(scores - lse_blocks[block_index])
        grad_block = grad_att_seq[:, row_low:row_high]
        grad_value_acc = grad_value_acc.at[:, :row_high].add(
            jnp.einsum(
                "shqk,sqhe->skhe",
                probs.astype(jnp.bfloat16),
                grad_block,
                preferred_element_type=jnp.float32,
            )
        )
        grad_probs = jnp.einsum(
            "sqhe,skhe->shqk",
            grad_block,
            value_seq[:, :row_high],
            preferred_element_type=jnp.float32,
        )
        grad_scores = probs * (grad_probs - jnp.sum(probs * grad_probs, axis=-1, keepdims=True))
        grad_scores_low = grad_scores.astype(jnp.bfloat16)
        content_grads.append(
            score_scale
            * jnp.einsum(
                "shqk,skhe->sqhe",
                grad_scores_low,
                key_seq[:, :row_high],
                preferred_element_type=jnp.float32,
            )
        )
        posq_grads.append(
            score_scale
            * jnp.einsum(
                "shqk,km->sqhm",
                grad_scores_low,
                key_feature[:row_high],
                preferred_element_type=jnp.float32,
            )
        )
        grad_key_acc = grad_key_acc.at[:, :row_high].add(
            score_scale
            * jnp.einsum(
                "shqk,sqhe->skhe",
                grad_scores_low,
                content_seq[:, row_low:row_high],
                preferred_element_type=jnp.float32,
            )
        )
    grad_content = jnp.concatenate(content_grads, axis=1).reshape(all_rows, head_count, head_size)
    grad_posq = jnp.concatenate(posq_grads, axis=1).reshape(all_rows, head_count, model_width)
    grad_pos_cos = grad_posq[:, :, :half_width]
    grad_pos_sin = grad_posq[:, :, half_width:]
    grad_coeffs = jnp.concatenate(
        [
            grad_pos_cos * sine_rows - grad_pos_sin * cosine_rows,
            grad_pos_cos * cosine_rows + grad_pos_sin * sine_rows,
        ],
        axis=-1,
    ).astype(jnp.bfloat16)
    grad_w_position = jnp.einsum(
        "shm,she->mhe", grad_coeffs, shift_heads, preferred_element_type=jnp.float32
    ).reshape(model_width, local_width)
    grad_shift = jnp.einsum(
        "shm,mhe->she", grad_coeffs, pos_weight, preferred_element_type=jnp.float32
    )
    grad_content_bias = jnp.sum(grad_content, axis=0)
    grad_position_bias = jnp.sum(grad_shift, axis=0)
    grad_query_low = (grad_content + grad_shift).reshape(all_rows, local_width).astype(jnp.bfloat16)
    grad_joint = jnp.concatenate(
        [
            grad_query_low,
            grad_key_acc.reshape(all_rows, local_width).astype(jnp.bfloat16),
            grad_value_acc.reshape(all_rows, local_width).astype(jnp.bfloat16),
        ],
        axis=1,
    )
    grad_w_joint = jnp.einsum("sd,se->de", norm_all, grad_joint, preferred_element_type=jnp.float32)
    grad_norm_own = lax.psum_scatter(
        jnp.einsum("se,de->sd", grad_joint, w_joint, preferred_element_type=jnp.float32).astype(
            jnp.bfloat16
        ),
        "mp",
        scatter_dimension=0,
        tiled=True,
    ).astype(jnp.float32)
    grad_in_full = grad_resid_own + norm_back(grad_norm_own, normed_one, inverse_one, gain_one)
    grad_gain_one = jnp.sum(grad_norm_own * normed_one, axis=0)
    grad_bias_one = jnp.sum(grad_norm_own, axis=0)
    grad_embed_part = jnp.einsum(
        "sv,sd->vd", one_hot.astype(jnp.float32), grad_in_full, precision=lax.Precision.HIGHEST
    )
    (
        sum_joint,
        sum_position,
        sum_content,
        sum_shift,
        sum_out,
        sum_up,
        sum_up_bias,
        sum_down,
        sum_pred,
        sum_pred_bias,
        sum_logit,
        sum_logit_bias,
        loss_total,
    ) = (
        lax.psum(grad_w_joint.astype(jnp.bfloat16), "dp").astype(jnp.float32),
        lax.psum(grad_w_position.astype(jnp.bfloat16), "dp").astype(jnp.float32),
        lax.psum(grad_content_bias.astype(jnp.bfloat16), "dp").astype(jnp.float32),
        lax.psum(grad_position_bias.astype(jnp.bfloat16), "dp").astype(jnp.float32),
        lax.psum(grad_w_out.astype(jnp.bfloat16), "dp").astype(jnp.float32),
        lax.psum(grad_w_up.astype(jnp.bfloat16), "dp").astype(jnp.float32),
        lax.psum(grad_up_bias.astype(jnp.bfloat16), "dp").astype(jnp.float32),
        lax.psum(grad_w_down.astype(jnp.bfloat16), "dp").astype(jnp.float32),
        lax.psum(grad_w_pred.astype(jnp.bfloat16), "dp").astype(jnp.float32),
        lax.psum(grad_pred_bias.astype(jnp.bfloat16), "dp").astype(jnp.float32),
        lax.psum(grad_w_logit.astype(jnp.bfloat16), "dp").astype(jnp.float32),
        lax.psum(grad_logit_bias.astype(jnp.bfloat16), "dp").astype(jnp.float32),
        lax.psum(loss_part.astype(jnp.bfloat16), "dp").astype(jnp.float32),
    )
    sum_embed, sum_gain_one, sum_bias_one, sum_gain_two, sum_bias_two, sum_down_bias = lax.psum(
        (
            grad_embed_part,
            grad_gain_one,
            grad_bias_one,
            grad_gain_two,
            grad_bias_two,
            grad_down_bias,
        ),
        ("dp", "mp"),
    )
    loss_value = loss_total / (all_rows * lax.axis_size("dp"))
    return (
        out_low_own,
        loss_value,
        grad_in_full.astype(jnp.bfloat16),
        sum_embed,
        sum_gain_one,
        sum_bias_one,
        sum_joint[:, :local_width],
        sum_joint[:, local_width : 2 * local_width],
        sum_joint[:, 2 * local_width :],
        sum_position,
        sum_content,
        sum_shift,
        sum_out,
        sum_gain_two,
        sum_bias_two,
        sum_up,
        sum_up_bias,
        sum_down,
        sum_down_bias,
        sum_pred,
        sum_pred_bias,
        sum_logit,
        sum_logit_bias,
    )


def solution(mesh):
    placed = (
        P(("dp", "mp")),
        P(),
        P("dp"),
        P(("dp", "mp"), None),
        P(),
        P(),
        P(None, "mp"),
        P(None, "mp"),
        P(None, "mp"),
        P(None, "mp"),
        P("mp", None),
        P("mp", None),
        P("mp", None),
        P(),
        P(),
        P(None, "mp"),
        P("mp"),
        P("mp", None),
        P(),
        P(None, "mp"),
        P("mp"),
        P("mp"),
        P(),
    )
    return jax.shard_map(
        per_device,
        mesh=mesh,
        in_specs=placed,
        out_specs=(
            P(("dp", "mp"), None),
            P(),
            P(("dp", "mp"), None),
            P(),
            P(),
            P(),
            P(None, "mp"),
            P(None, "mp"),
            P(None, "mp"),
            P(None, "mp"),
            P("mp", None),
            P("mp", None),
            P("mp", None),
            P(),
            P(),
            P(None, "mp"),
            P("mp"),
            P("mp", None),
            P(),
            P(None, "mp"),
            P("mp"),
            P("mp"),
            P(),
        ),
        check_vma=False,
    )
```

profile of v0, /device:TPU:0, one launch (start us, length us, event | category | flops | bytes accessed | tf_op | source)
XLA Modules:
  0.0 833.0 jit_solution(15598323254271933989)
XLA Ops:
  12.8 9.1 %fusion.108 = (f32[2048,256]{1,0:T(8,128)}, bf16[2048,256]{1,0:T(8,128)(2,1)S(1)}, bf16[2048,256]{1,0:T(8,128)(2,1)}, f32[2048,256]{1,0:T(8,128)}) fusion(f32[256]{0:T(256)S(1)} %multiply_exponential_fusion), kind=kLoop, calls=%fused_computation.178 | loop fusion | flops 1572864 | bytes 6292480 | tf_op jit(solution)/shard_map/sin | solution.py:41
  21.9 3.4 copy.80
  25.2 2.9 copy.81
  32.6 28.6 %all-gather.2.cloned.1.call-done = bf16[2048,512]{0,1:T(8,128)(2,1)} async-done(((bf16[512,512]{0,1:T(8,128)(2,1)}), bf16[2048,512]{0,1:T(8,128)(2,1)}) %all-gather.2.cloned.1.call-update) | async-done | bytes 2097168 | tf_op jit(solution)/shard_map/all_gather | solution.py:97
  74.0 4.3 fusion.242
  82.3 3.1 fusion.241
  88.2 4.5 fusion.209
  92.7 6.1 fusion.240
  107.0 8.8 %all-reduce.14.cloned.1.call-start = ((), (), s32[]{:S(2)}) async-start(), calls=%async_computation.3 | async-start | bytes 4194304 | tf_op jit(solution)/shard_map/psum | solution.py:183
  115.9 76.5 %all-reduce.12.cloned.1.call-done = bf16[2048,512]{0,1:T(8,128)(2,1)} async-done(((bf16[2048,512]{0,1:T(8,128)(2,1)}), bf16[2048,512]{0,1:T(8,128)(2,1)}) %all-reduce.12.cloned.1.call-update) | async-done | bytes 2097168 | tf_op jit(solution)/shard_map/psum | solution.py:172
  196.7 13.0 %fusion.19 = (bf16[2048,512]{1,0:T(8,128)(2,1)S(1)}, f32[2048,512]{1,0:T(8,128)}) fusion(f32[512]{0:T(512)S(1)} %convert_element_type.348, bf16[512,512]{1,0:T(8,128)(2,1)} %param.58, f32[512]{0:T(512)S(1)} %convert_element_type.346, f32[512]{0:T(512)S(1)} %convert_element_type.345, f32[2048]{0:T(1024)S(1)} %add_rsqrt_fusion, ...), kind=kOutput, calls=%fused_computation.46 | convolution fusion | flops 1149239296 | bytes 8935424 | tf_op jit(solution)/shard_map/dot_general | solution.py:176
  211.1 3.0 convolution_convert_fusion.2
  216.9 82.8 %all-reduce.14.cloned.1.call-done = bf16[2048,512]{0,1:T(8,128)(2,1)} async-done(((bf16[2048,512]{0,1:T(8,128)(2,1)}), bf16[2048,512]{0,1:T(8,128)(2,1)}) %all-reduce.14.cloned.1.call-update) | async-done | bytes 2097168 | tf_op jit(solution)/shard_map/psum | solution.py:183
  301.9 11.0 %fusion.22 = (bf16[2048,512]{1,0:T(8,128)(2,1)S(1)}, f32[2048,512]{1,0:T(8,128)}) fusion(f32[512]{0:T(512)S(1)} %convert_element_type.354, bf16[2048,512]{0,1:T(8,128)(2,1)S(1)} %fusion.16, bf16[512,512]{1,0:T(8,128)(2,1)S(1)} %copy-done), kind=kOutput, calls=%fused_computation.49 | convolution fusion | flops 1142947840 | bytes 8914944 | tf_op jit(solution)/shard_map/dot_general | solution.py:187
  315.0 9.9 %psum.170 = f32[2048]{0:T(1024)S(1)} all-reduce(f32[2048]{0:T(1024)S(1)} %bitcast.500), channel_id=1, replica_groups=mesh['dp'=8,'mp'=4] {'mp'}, use_global_device_ids=true, to_apply=%region_14.15 | all-reduce | flops 2048 | bytes 16384 | tf_op jit(solution)/shard_map/psum | solution.py:192
  325.5 4.4 fusion.232
  333.4 84.8 %all-reduce.16.cloned.1.call-done = bf16[2048,512]{0,1:T(8,128)(2,1)} async-done(((bf16[2048,512]{0,1:T(8,128)(2,1)}), bf16[2048,512]{0,1:T(8,128)(2,1)}) %all-reduce.16.cloned.1.call-update) | async-done | bytes 2097168 | tf_op jit(solution)/shard_map/psum | solution.py:211
  418.2 5.1 fusion.248
  428.0 4.4 convolution_convert_fusion.4
  436.6 76.4 %all-reduce.18.cloned.1.call-done = bf16[2048,512]{0,1:T(8,128)(2,1)} async-done(((bf16[2048,512]{0,1:T(8,128)(2,1)}), bf16[2048,512]{0,1:T(8,128)(2,1)}) %all-reduce.18.cloned.1.call-update) | async-done | bytes 2097168 | tf_op jit(solution)/shard_map/psum | solution.py:222
  513.0 5.0 multiply_reduce_fusion.1
  541.5 3.2 multiply_bitcast_fusion.1
  544.7 4.2 fusion.3
  548.9 4.6 fusion.36
  555.6 3.7 multiply_bitcast_fusion
  580.1 3.9 convolution_convert_fusion
  589.1 14.6 %all-reduce.3 = (bf16[1]{0:T(256)(128)(2,1)}, bf16[2,64]{1,0:T(2,128)(2,1)S(1)}, bf16[2,64]{1,0:T(2,128)(2,1)S(1)}, bf16[512]{0:T(512)(128)(2,1)S(1)}, bf16[512]...) all-reduce(bf16[1]{0:T(256)(128)(2,1)} %bitcast.55, ...), channel_id=1, replica_groups=mesh['dp'=8,'mp'=4] {'dp'}, use_global_device_ids=true, to_apply=%region_16.17 | all-reduce | flops 1794 | bytes 7176 | tf_op jit(solution)/shard_map/psum | solution.py:359
  610.1 32.7 %all-reduce.22.cloned.1.call-done = (bf16[512,384]{1,0:T(8,128)(2,1)}, bf16[512,128]{1,0:T(8,128)(2,1)}, bf16[128,512]{1,0:T(8,128)(2,1)}, bf16[512,512]{1,0:T(8...) async-done(((bf16[512,384]{1,0:T(8,128)(2,1)}, bf16[512,128]{1,0:T(8,128)(2,1)}, bf16[128,512]{1,0:T(8,128)(2,1)}, bf16[512,512]{1,0:T(8,128)(2,1)}, ...) | async-done | bytes 2228240 | tf_op jit(solution)/shard_map/psum | solution.py:347
  652.4 36.1 %reduce-scatter.2.cloned.1.call-done = bf16[512,512]{0,1:T(8,128)(2,1)} async-done(((bf16[2048,512]{0,1:T(8,128)(2,1)}), bf16[512,512]{0,1:T(8,128)(2,1)}) %reduce-scatter.2.cloned.1.call-update) | async-done | bytes 524304 | tf_op jit(solution)/shard_map/reduce_scatter | solution.py:318
  690.2 3.4 fusion.197
  696.2 39.8 %all-reduce.2 = (f32[512]{0:T(512)}, f32[512]{0:T(512)}, f32[512]{0:T(512)}, f32[512]{0:T(512)}, f32[512]{0:T(512)}) all-reduce(f32[512]{0:T(512)S(1)} %get-tuple-element.185, f32[512]{0:T(512)S(1)} %get-tuple-element.188, f32[512]{0:T(512)S(1)} %get-tuple-element.182, ...), channel_id=1, replica_groups=mesh['dp'=8,'mp'=4] {'dp','mp'}, use_global_device_ids=true, to_apply=%region_30.31 | all-reduce | flops 2560 | bytes 20480 | tf_op jit(solution)/shard_map/psum | solution.py:361
  736.0 85.6 %all-reduce.20.cloned.1.call-done = f32[256,512]{1,0:T(8,128)} async-done(((f32[256,512]{1,0:T(8,128)}), f32[256,512]{1,0:T(8,128)}) %all-reduce.20.cloned.1.call-update) | async-done | bytes 524304 | tf_op jit(solution)/shard_map/psum | solution.py:361
  (333 shorter events, 133.7 us)
Async XLA Ops:
  7.2 294.7 %copy-start = (bf16[512,512]{1,0:T(8,128)(2,1)S(1)}, bf16[512,512]{1,0:T(8,128)(2,1)}, u32[]{:S(2)}) copy-start(bf16[512,512]{1,0:T(8,128)(2,1)} %param.62) | copy-start | bytes 1572868
  7.2 54.0 %all-gather.2.cloned.1.call-start = ((), (), s32[]{:S(2)}) async-start(), calls=%async_computation.1 | async-start | bytes 2621440 | tf_op jit(solution)/shard_map/all_gather | solution.py:97
  10.2 94.9 %copy-start.9 = (f32[512,512]{0,1:T(8,128)}, f32[512,512]{0,1:T(8,128)S(1)}, u32[]{:S(2)}) copy-start(f32[512,512]{0,1:T(8,128)S(1)} %get-tuple-element.234) | copy-start | bytes 3145732
  12.4 180.0 %all-reduce.12.cloned.1.call-start = ((), (), s32[]{:S(2)}) async-start(), calls=%async_computation.2 | async-start | bytes 4194304 | tf_op jit(solution)/shard_map/psum | solution.py:172
  12.8 56.9 %copy-start.54 = (bf16[512,128]{0,1:T(8,128)(2,1)}, bf16[512,128]{0,1:T(8,128)(2,1)S(1)}, u32[]{:S(2)}) copy-start(bf16[512,128]{0,1:T(8,128)(2,1)S(1)} %copy.79) | copy-start | bytes 393220
  21.9 70.9 %copy-start.12 = (bf16[2048,256]{1,0:T(8,128)(2,1)}, bf16[2048,256]{1,0:T(8,128)(2,1)S(1)}, u32[]{:S(2)}) copy-start(bf16[2048,256]{1,0:T(8,128)(2,1)S(1)} %get-tuple-element.230) | copy-start | bytes 3145732
  28.3 35.5 %copy-start.52 = (bf16[512,384]{1,0:T(8,128)(2,1)}, bf16[512,384]{1,0:T(8,128)(2,1)S(1)}, u32[]{:S(2)}) copy-start(bf16[512,384]{1,0:T(8,128)(2,1)S(1)} %constant_dynamic-update-slice_fusion) | copy-start | bytes 1179652
  64.0 24.2 %copy-start.20 = (bf16[2048,128]{0,1:T(8,128)(2,1)}, bf16[2048,128]{0,1:T(8,128)(2,1)S(1)}, u32[]{:S(2)}) copy-start(bf16[2048,128]{0,1:T(8,128)(2,1)S(1)} %get-tuple-element.220) | copy-start | bytes 1572868
  64.2 24.0 %copy-start.37 = (bf16[2048,128]{0,1:T(8,128)(2,1)}, bf16[2048,128]{0,1:T(8,128)(2,1)S(1)}, u32[]{:S(2)}) copy-start(bf16[2048,128]{0,1:T(8,128)(2,1)S(1)} %get-tuple-element.218) | copy-start | bytes 1572868
  105.3 10.5 %copy-start.76 = (bf16[512]{0:T(512)(128)(2,1)S(1)}, bf16[512]{0:T(512)(128)(2,1)}, u32[]{:S(2)}) copy-start(bf16[512]{0:T(512)(128)(2,1)} %param.56) | copy-start | bytes 3076
  105.3 10.5 %copy-start.77 = (bf16[512]{0:T(512)(128)(2,1)S(1)}, bf16[512]{0:T(512)(128)(2,1)}, u32[]{:S(2)}) copy-start(bf16[512]{0:T(512)(128)(2,1)} %param.57) | copy-start | bytes 3076
  105.4 10.5 %copy-start.78 = (bf16[512]{0:T(512)(128)(2,1)S(1)}, bf16[512]{0:T(512)(128)(2,1)}, u32[]{:S(2)}) copy-start(bf16[512]{0:T(512)(128)(2,1)} %param.59) | copy-start | bytes 3076
  107.0 192.6 %all-reduce.14.cloned.1.call-start = ((), (), s32[]{:S(2)}) async-start(), calls=%async_computation.3 | async-start | bytes 4194304 | tf_op jit(solution)/shard_map/psum | solution.py:183
  196.7 14.3 %copy-start.81 = (bf16[512,512]{1,0:T(8,128)(2,1)S(1)}, bf16[512,512]{1,0:T(8,128)(2,1)}, u32[]{:S(2)}) copy-start(bf16[512,512]{1,0:T(8,128)(2,1)} %param.60) | copy-start | bytes 1572868
  214.0 204.2 %all-reduce.16.cloned.1.call-start = ((), (), s32[]{:S(2)}) async-start(), calls=%async_computation.4 | async-start | bytes 4194304 | tf_op jit(solution)/shard_map/psum | solution.py:211
  301.9 11.1 %copy-start.40 = (bf16[2048,512]{0,1:T(8,128)(2,1)}, bf16[2048,512]{0,1:T(8,128)(2,1)S(1)}, u32[]{:S(2)}) copy-start(bf16[2048,512]{0,1:T(8,128)(2,1)S(1)} %fusion.16) | copy-start | bytes 6291460
  301.9 23.0 %copy-start.73 = (s32[2048]{0:T(1024)S(1)}, s32[2048]{0:T(1024)}, u32[]{:S(2)}) copy-start(s32[2048]{0:T(1024)} %param.45) | copy-start | bytes 24580
  331.6 86.6 %copy-start.82 = (bf16[512,512]{1,0:T(8,128)(2,1)S(1)}, bf16[512,512]{1,0:T(8,128)(2,1)}, u32[]{:S(2)}) copy-start(bf16[512,512]{1,0:T(8,128)(2,1)} %param.60) | copy-start | bytes 1572868
  333.3 179.7 %all-reduce.18.cloned.1.call-start = ((), (), s32[]{:S(2)}) async-start(), calls=%async_computation.5 | async-start | bytes 4194304 | tf_op jit(solution)/shard_map/psum | solution.py:222
  427.4 215.4 %all-reduce.22.cloned.1.call-start = ((), (), s32[]{:S(2)}) async-start(), calls=%async_computation.8 | async-start | bytes 4456448 | tf_op jit(solution)/shard_map/psum | solution.py:347
  579.8 6.5 copy-start.30
  579.8 108.7 %reduce-scatter.2.cloned.1.call-start = ((), (), s32[]{:S(2)}) async-start(), calls=%async_computation.6 | async-start | bytes 2621440 | tf_op jit(solution)/shard_map/reduce_scatter | solution.py:318
  584.0 237.6 %all-reduce.20.cloned.1.call-start = ((), (), s32[]{:S(2)}) async-start(), calls=%async_computation.7 | async-start | bytes 1048576 | tf_op jit(solution)/shard_map/psum | solution.py:361
  586.6 21.3 %copy-start.17 = (bf16[2048,512]{0,1:T(8,128)(2,1)S(1)}, bf16[2048,512]{0,1:T(8,128)(2,1)}, u32[]{:S(2)}) copy-start(bf16[2048,512]{0,1:T(8,128)(2,1)} %all-reduce.18.cloned.1.call-done) | copy-start | bytes 6291460
  608.4 80.0 %copy-start.10 = (f32[512,512]{0,1:T(8,128)S(1)}, f32[512,512]{0,1:T(8,128)}, u32[]{:S(2)}) copy-start(f32[512,512]{0,1:T(8,128)} %copy-done.9) | copy-start | bytes 3145732
  608.5 80.0 %copy-start.64 = (f32[512]{0:T(512)S(1)}, f32[512]{0:T(512)}, u32[]{:S(2)}) copy-start(f32[512]{0:T(512)} %copy-done.63) | copy-start | bytes 6148
  608.5 80.0 %copy-start.66 = (f32[512]{0:T(512)S(1)}, f32[512]{0:T(512)}, u32[]{:S(2)}) copy-start(f32[512]{0:T(512)} %copy-done.65) | copy-start | bytes 6148
  608.5 80.0 %copy-start.68 = (f32[512]{0:T(512)S(1)}, f32[512]{0:T(512)}, u32[]{:S(2)}) copy-start(f32[512]{0:T(512)} %copy-done.67) | copy-start | bytes 6148
  642.8 7.6 copy-start.56
  642.8 8.7 %copy-start.50 = (bf16[512,384]{1,0:T(8,128)(2,1)S(1)}, bf16[512,384]{1,0:T(8,128)(2,1)}, u32[]{:S(2)}) copy-start(bf16[512,384]{1,0:T(8,128)(2,1)} %get-tuple-element.203) | copy-start | bytes 1179652
  644.5 45.7 %copy-start.74 = (s32[512]{0:T(512)S(1)}, s32[512]{0:T(512)}, u32[]{:S(2)}) copy-start(s32[512]{0:T(512)} %param.43) | copy-start | bytes 6148
  690.1 133.4 %copy-start.1 = (bf16[512,512]{1,0:T(8,128)(2,1)S(1)}, bf16[512,512]{1,0:T(8,128)(2,1)}, u32[]{:S(2)}) copy-start(bf16[512,512]{1,0:T(8,128)(2,1)} %param.62) | copy-start | bytes 1572868
  (71 other events, 223.9 us)
Sparse Core Ops, SparseCore 0:
  12.5 48.6 all-gather.1
  107.2 85.2 all-reduce.11
  214.2 85.4 all-reduce.13
  333.4 84.7 all-reduce.15
  427.5 85.4 all-reduce.17
  579.9 62.8 all-reduce.21
  645.2 43.2 reduce-scatter.1
  694.3 127.2 all-reduce.19
where the time goes:
time: 841 us; the launch traced here: 833 us
  waiting for transfers between devices  504 us (60%)
  matrix products  133 us (16%)
  other arithmetic  73.4 us (9%)
  blocking collectives  64.3 us (8%)
  local copies, waits for them, and re-layouts  29.1 us (3%)
  between operations  20.2 us (2%)
  starting transfers between devices  9.73 us (1%)
    psum x1, waiting for transfers between devices, per_device(): lax.psum((grad_embed_part, grad_gain_one, grad_bias_one, grad_gain_two, g...  85.6 us
    psum x1, waiting for transfers between devices, per_device(): lax.psum(pred_back.astype(jnp.bfloat16), 'mp').astype(jnp.float32)  84.8 us
    psum x1, waiting for transfers between devices, per_device(): lax.psum(ffn_part.astype(jnp.bfloat16), 'mp').astype(jnp.float32)  82.8 us
    psum x1, waiting for transfers between devices, per_device(): middle = lax.psum(attn_part.astype(jnp.bfloat16), 'mp').astype(jnp.float32)  76.5 us
    psum x1, waiting for transfers between devices, per_device(): lax.psum(grad_mid_part.astype(jnp.bfloat16), 'mp').astype(jnp.float32)  76.4 us
    psum x1, blocking collectives, per_device(): lax.psum((grad_embed_part, grad_gain_one, grad_bias_one, grad_gain_two, g...  39.8 us
    reduce_scatter x1, waiting for transfers between devices, per_device(): lax.psum_scatter(jnp.einsum('se,de->sd', grad_joint, w_joint, preferred_e...  36.1 us
    psum x1, waiting for transfers between devices, per_device(): lax.psum(grad_w_joint.astype(jnp.bfloat16), 'dp').astype(jnp.float32)  32.7 us
  transfers between devices with their start and end apart: 8, of which 8 were waited for; matrix products, arithmetic and copies ran while one was open for 7% of the time, Pallas kernels for 0%

commit v1 on v0

v1 whole, which is shorter than its diff:
```python
import functools
import math

import jax
import jax.numpy as jnp
import numpy as np
from jax import lax
from jax.experimental import pallas as pl
from jax.experimental.pallas import tpu as pltpu
from jax.sharding import PartitionSpec as P

LEN = 2048
BLOCK = 256
VMEM_BYTES = 56 * 1024 * 1024

bf16 = jnp.bfloat16
f32 = jnp.float32
norm_eps = 1e-05
density_scale = 1.0 / math.sqrt(2.0 * math.pi)
log2_e = math.log2(math.e)


def nn(first, second):
    return jnp.dot(first, second, preferred_element_type=f32)


def nt(first, second):
    return lax.dot_general(
        first, second, (((1,), (1,)), ((), ())), preferred_element_type=f32
    )


def tn(first, second):
    return lax.dot_general(
        first, second, (((0,), (0,)), ((), ())), preferred_element_type=f32
    )


def layer_stats(values):
    centered = values - jnp.mean(values, axis=-1, keepdims=True)
    inverse = lax.rsqrt(jnp.mean(centered * centered, axis=-1, keepdims=True) + norm_eps)
    return centered * inverse, inverse


def norm_back(grad_normed, normed, inverse, gain_row):
    scaled = grad_normed * gain_row
    first_mean = jnp.mean(scaled, axis=-1, keepdims=True)
    second_mean = jnp.mean(scaled * normed, axis=-1, keepdims=True)
    return inverse * (scaled - first_mean - normed * second_mean)


def gelu_parts(values):
    size = jnp.abs(values)
    fall = jnp.exp(-0.5 * values * values)
    t = 1.0 / (1.0 + (0.3275911 / math.sqrt(2.0)) * size)
    poly = 1.061405429 * t - 1.453152027
    poly = poly * t + 1.421413741
    poly = poly * t - 0.284496736
    poly = poly * t + 0.254829592
    tail = 0.5 * poly * t * fall
    phi = jnp.where(values >= 0, 1.0 - tail, tail)
    return values * phi, phi + values * fall * density_scale


def feature_tables(model_width):
    half = model_width // 2
    frequency = np.exp(
        np.arange(half, dtype=np.float64) * (-2.0 * math.log(10000.0) / model_width)
    )
    angles = np.arange(LEN, dtype=np.float64)[:, None] * frequency[None, :]
    return np.sin(angles).astype(np.float32), np.cos(angles).astype(np.float32)


def embed_rows(ids_row, table):
    vocab = table.shape[0]
    places = lax.broadcasted_iota(jnp.int32, (vocab, ids_row.shape[1]), 0)
    one_hot_t = (places == ids_row).astype(f32)
    rows = nn(one_hot_t.T.astype(bf16), table)
    return one_hot_t, rows


def full(shape):
    return pl.BlockSpec(shape, lambda *_: (0,) * len(shape))


def params():
    return pltpu.CompilerParams(vmem_limit_bytes=VMEM_BYTES)


def pre_kernel(mp, heads, score_scale, me_ref, *refs):
    id_refs = refs[:mp]
    (table, gain, bias, w_joint, w_pos, c_bias, p_bias, feature, feature_t, sines, cosines) = refs[
        mp : mp + 11
    ]
    norm_out, qcat, kcat, kcat_t, v_out, v_t, shift_out, ids_s = refs[mp + 11 :]
    step = pl.program_id(0)
    me = me_ref[0]
    own = id_refs[0].shape[1]

    @pl.when(step == 0)
    def _():
        for k in range(mp):
            source = lax.rem(me - k + mp, mp)
            ids_s[:, pl.ds(pl.multiple_of(source * own, own), own)] = id_refs[k][...]

    rows = norm_out.shape[0]
    ids = ids_s[:, pl.ds(pl.multiple_of(step * rows, rows), rows)]
    _, inputs = embed_rows(ids, table[...])
    normed, _ = layer_stats(inputs)
    norm_in = (normed * gain[...] + bias[...]).astype(bf16)
    norm_out[...] = norm_in
    joint = nn(norm_in, w_joint[...])
    width = v_out.shape[1]
    head_size = width // heads
    raw = joint[:, :width]
    keys = joint[:, width : 2 * width].astype(bf16)
    values = joint[:, 2 * width :].astype(bf16)
    v_out[...] = values
    v_t[...] = values.astype(f32).T.astype(bf16)
    model = feature.shape[1]
    half = model // 2
    kcat[:, :model] = feature[...]
    kcat[:, model:] = keys
    keys_t = keys.astype(f32).T.astype(bf16)
    kcat_t[:head_size] = keys_t[:head_size]
    kcat_t[head_size : head_size + model] = feature_t[...]
    if heads > 1:
        kcat_t[head_size + model :] = keys_t[head_size:]
    shift = (raw + p_bias[...]).astype(bf16)
    shift_out[...] = shift
    fold = score_scale * log2_e
    content = (raw + c_bias[...]) * fold
    lane = lax.broadcasted_iota(jnp.int32, content.shape, 1)
    sin, cos = sines[...], cosines[...]
    for h in range(heads):
        low, high = h * head_size, (h + 1) * head_size
        coeffs = nt(shift[:, low:high], w_pos[:, low:high])
        c_sin, c_cos = coeffs[:, :half] * fold, coeffs[:, half:] * fold
        qcat[h, :, :half] = (c_sin * sin + c_cos * cos).astype(bf16)
        qcat[h, :, half:model] = (c_cos * sin - c_sin * cos).astype(bf16)
        mine = (lane >= low) & (lane < high)
        qcat[h, :, model:] = jnp.where(mine, content, 0.0).astype(bf16)


def pre_call(me, id_parts, table, gain, bias, w_joint, w_pos, c_bias, p_bias, tables, heads, scale):
    mp = len(id_parts)
    own = id_parts[0].shape[1]
    model = table.shape[1]
    width = w_pos.shape[1]
    rows = BLOCK
    feature, feature_t, sines, cosines = tables
    cat = model + width
    row_block = lambda n: pl.BlockSpec((rows, n), lambda i, m: (i, 0))
    col_block = lambda n: pl.BlockSpec((n, rows), lambda i, m: (0, i))
    ins = [*id_parts, table, gain, bias, w_joint, w_pos, c_bias, p_bias]
    return pl.pallas_call(
        functools.partial(pre_kernel, mp, heads, scale),
        grid_spec=pltpu.PrefetchScalarGridSpec(
            num_scalar_prefetch=1,
            grid=(LEN // rows,),
            in_specs=[full(a.shape) for a in ins]
            + [row_block(model), col_block(model), row_block(model // 2), row_block(model // 2)],
            out_specs=[
                row_block(model),
                pl.BlockSpec((heads, rows, cat), lambda i, m: (0, i, 0)),
                row_block(cat),
                col_block(cat),
                row_block(width),
                col_block(width),
                row_block(width),
            ],
            scratch_shapes=[pltpu.VMEM((1, mp * own), jnp.int32)],
        ),
        out_shape=[
            jax.ShapeDtypeStruct((LEN, model), bf16),
            jax.ShapeDtypeStruct((heads, LEN, cat), bf16),
            jax.ShapeDtypeStruct((LEN, cat), bf16),
            jax.ShapeDtypeStruct((cat, LEN), bf16),
            jax.ShapeDtypeStruct((LEN, width), bf16),
            jax.ShapeDtypeStruct((width, LEN), bf16),
            jax.ShapeDtypeStruct((LEN, width), bf16),
        ],
        compiler_params=params(),
        cost_estimate=pl.CostEstimate(
            flops=2 * LEN * model * (table.shape[0] + 4 * width), bytes_accessed=24 << 20, transcendentals=0
        ),
        name="project",
    )(me, *ins, feature, feature_t, sines, cosines)


def fwd_kernel(mp, own, me_ref, qcat, kcat, v_t, expon_out, full_t, inv_out, *piece_refs):
    step = pl.program_id(0)
    me = me_ref[0]
    rows = qcat.shape[1]
    for block in range(LEN // rows):

        @pl.when(step == block)
        def _(block=block):
            low, high = block * rows, (block + 1) * rows
            queries = qcat[0]
            last = nt(kcat[low:high], queries)
            key_place = lax.broadcasted_iota(jnp.int32, last.shape, 0)
            query_place = lax.broadcasted_iota(jnp.int32, last.shape, 1)
            last = jnp.where(key_place <= query_place, last, -1e30)
            top = jnp.max(last, axis=0, keepdims=True)
            if block:
                first = nt(kcat[:low], queries)
                top = jnp.maximum(top, jnp.max(first, axis=0, keepdims=True))
            e_last = jnp.exp2(last - top)
            total = jnp.sum(e_last, axis=0, keepdims=True)
            e_last = e_last.astype(bf16)
            expon_out[0, low:high] = e_last
            mixed = nn(v_t[:, low:high], e_last)
            if block:
                e_first = jnp.exp2(first - top)
                total = total + jnp.sum(e_first, axis=0, keepdims=True)
                e_first = e_first.astype(bf16)
                expon_out[0, :low] = e_first
                mixed = mixed + nn(v_t[:, :low], e_first)
            inverse = 1.0 / total
            inv_out[...] = inverse
            mixed = mixed * inverse
            full_t[...] = mixed
            relative = lax.rem(low // own - me + mp, mp)
            start = low % own
            for k in range(mp):

                @pl.when(relative == k)
                def _(k=k):
                    piece_refs[k][:, start : start + rows] = mixed.astype(bf16)


def fwd_call(me, head, qcat, kcat, v_t, mp, own, head_size):
    rows = min(BLOCK, own)
    blocks = LEN // rows
    cat = kcat.shape[1]
    return pl.pallas_call(
        functools.partial(fwd_kernel, mp, own),
        grid_spec=pltpu.PrefetchScalarGridSpec(
            num_scalar_prefetch=1,
            grid=(blocks,),
            in_specs=[
                pl.BlockSpec((1, rows, cat), lambda i, m: (head, i, 0)),
                full(kcat.shape),
                pl.BlockSpec((head_size, LEN), lambda i, m: (head, 0)),
            ],
            out_specs=[
                pl.BlockSpec((1, LEN, rows), lambda i, m: (i, 0, 0)),
                pl.BlockSpec((head_size, rows), lambda i, m: (0, i)),
                pl.BlockSpec((1, rows), lambda i, m: (0, i)),
            ]
            + [full((head_size, own))] * mp,
        ),
        out_shape=[
            jax.ShapeDtypeStruct((blocks, LEN, rows), bf16),
            jax.ShapeDtypeStruct((head_size, LEN), f32),
            jax.ShapeDtypeStruct((1, LEN), f32),
        ]
        + [jax.ShapeDtypeStruct((head_size, own), bf16)] * mp,
        compiler_params=params(),
        cost_estimate=pl.CostEstimate(
            flops=2 * LEN * LEN * (cat + head_size) * 6 // 10,
            bytes_accessed=16 << 20,
            transcendentals=LEN * LEN * 6 // 10,
        ),
        name="attend",
    )(me, qcat, kcat, v_t)


def bwd_kernel(mp, own, head, heads, score_scale, me_ref, *refs):
    g_refs = refs[:mp]
    (expon, full_t, inv, slot, kcat_t, v, shift, w_pos_t, sin_t, cos_t, norm_all) = refs[mp : mp + 11]
    out = refs[mp + 11 :]
    piece_refs = out[:mp]
    dw_out, dpos, dcb, dpb = out[mp : mp + 4]
    grad_s, dk_s, dv_s, all_s = out[mp + 4 :]
    step = pl.program_id(0)
    steps = pl.num_programs(0)
    me = me_ref[0]
    rows = inv.shape[1]
    size = full_t.shape[0]
    width = v.shape[1]
    model = w_pos_t.shape[1]
    half = model // 2
    first_row = head * size

    @pl.when(step == 0)
    def _():
        for k in range(mp):
            source = lax.rem(me - k + mp, mp)
            grad_s[:, pl.ds(pl.multiple_of(source * own, own), own)] = g_refs[k][...]
        dk_s[...] = jnp.zeros_like(dk_s)
        dv_s[...] = jnp.zeros_like(dv_s)
        dpos[...] = jnp.zeros_like(dpos)
        dcb[...] = jnp.zeros_like(dcb)
        dpb[...] = jnp.zeros_like(dpb)

    def masked_rows(part):
        if heads == 1:
            return part
        zeros = jnp.zeros((size, part.shape[1]), part.dtype)
        return jnp.concatenate([part if h == head else zeros for h in range(heads)], axis=0)

    for block in range(LEN // rows):

        @pl.when(step == block)
        def _(block=block):
            low, high = block * rows, (block + 1) * rows
            grad = grad_s[:, low:high].astype(f32) * inv[...]
            delta = jnp.sum(grad * full_t[...], axis=0, keepdims=True)
            grad = masked_rows(grad)
            grad_t = grad.astype(bf16)
            grad_n = grad.T.astype(bf16)
            exp_all = expon[0, :high]
            grad_probs = nn(v[:high], grad_t)
            grad_scores = (exp_all.astype(f32) * (grad_probs - delta)).astype(bf16)
            dv_s[:high] += nn(exp_all, grad_n)
            dk_s[:high] += nn(grad_scores, slot[0])
            joint = nn(kcat_t[first_row : first_row + size + model, :high], grad_scores)
            joint = joint * score_scale
            if head == 0:
                d_content, d_pos = joint[:size], joint[size:]
            else:
                d_content, d_pos = joint[model:], joint[:model]
            g_cos, g_sin = d_pos[:half], d_pos[half:]
            sin, cos = sin_t[...], cos_t[...]
            d_coeff = jnp.concatenate(
                [
                    (g_cos * sin - g_sin * cos).astype(bf16),
                    (g_cos * cos + g_sin * sin).astype(bf16),
                ],
                axis=0,
            )
            dpos[...] += nn(d_coeff, shift[...])
            d_shift = nn(w_pos_t[...], d_coeff)
            dcb[...] += jnp.sum(d_content, axis=1, keepdims=True)
            dpb[...] += jnp.sum(d_shift, axis=1, keepdims=True)
            all_s[:size, low:high] = (d_content + d_shift).astype(bf16)

    @pl.when(step == steps - 1)
    def _():
        mine = slice(first_row, first_row + size)
        all_s[size : 2 * size] = (dk_s[...] * (1.0 / log2_e)).T[mine].astype(bf16)
        all_s[2 * size :] = dv_s[...].T[mine].astype(bf16)
        dw_out[...] = nn(all_s[...], norm_all[...]).astype(bf16)
        for k in range(mp):
            target = lax.rem(me + k, mp)
            piece_refs[k][...] = all_s[:, pl.ds(pl.multiple_of(target * own, own), own)]


def bwd_call(
    me, head, heads, pieces, expon, full_t, inv, qcat, kcat_t, v, shift, w_pos, tables_t, norm_all, scale
):
    mp = len(pieces)
    size, own = pieces[0].shape
    blocks, _, rows = expon.shape
    width = v.shape[1]
    model = norm_all.shape[1]
    col_block = lambda n: pl.BlockSpec((n, rows), lambda i, m: (0, i))
    if width % 128 == 0:
        slot, slot_spec = qcat, pl.BlockSpec((1, rows, width), lambda i, m: (head, i, model // width))
    else:
        slot, slot_spec = qcat[:, :, model:], pl.BlockSpec((1, rows, width), lambda i, m: (head, i, 0))
    w_pos_t = w_pos[:, head * size : (head + 1) * size].T
    return pl.pallas_call(
        functools.partial(bwd_kernel, mp, own, head, heads, scale),
        grid_spec=pltpu.PrefetchScalarGridSpec(
            num_scalar_prefetch=1,
            grid=(blocks,),
            in_specs=[full((size, own))] * mp
            + [
                pl.BlockSpec((1, LEN, rows), lambda i, m: (i, 0, 0)),
                col_block(size),
                col_block(1),
                slot_spec,
                full(kcat_t.shape),
                full(v.shape),
                pl.BlockSpec((rows, width), lambda i, m: (i, 0)),
                full(w_pos_t.shape),
                col_block(model // 2),
                col_block(model // 2),
                full(norm_all.shape),
            ],
            out_specs=[full((3 * size, own))] * mp
            + [full((3 * size, model)), full((model, width)), full((size, 1)), full((size, 1))],
            scratch_shapes=[
                pltpu.VMEM((size, LEN), bf16),
                pltpu.VMEM((LEN, width), f32),
                pltpu.VMEM((LEN, width), f32),
                pltpu.VMEM((3 * size, LEN), bf16),
            ],
        ),
        out_shape=[jax.ShapeDtypeStruct((3 * size, own), bf16)] * mp
        + [
            jax.ShapeDtypeStruct((3 * size, model), bf16),
            jax.ShapeDtypeStruct((model, width), f32),
            jax.ShapeDtypeStruct((size, 1), f32),
            jax.ShapeDtypeStruct((size, 1), f32),
        ],
        compiler_params=params(),
        cost_estimate=pl.CostEstimate(
            flops=2 * LEN * LEN * (model + 4 * width) * 6 // 10, bytes_accessed=24 << 20, transcendentals=0
        ),
        name="attend_back",
    )(me, *pieces, expon, full_t, inv, slot, kcat_t, v, shift, w_pos_t, *tables_t, norm_all)


def rows_kernel(mp, heads, me_ref, *refs):
    count = heads * mp
    pieces = refs[:count]
    (ids, labels, cotangent, table, w_out, gain, bias, down_bias, logit_bias, vec, w_up, w_down, w_pred) = refs[
        count : count + 13
    ]
    out = refs[count + 13 :]
    back = out[:count]
    (block_out, grad_mid, d_up, d_down, d_pred, d_out, d_vec, d_norm, d_scalar) = out[count : count + 9]
    (att, xhat, inv, norm_mid, norm_mid_t, total, out_low, out_low_t, hidden, slope, p_hidden, p_slope, logit, g_logit) = out[
        count + 9 :
    ]
    step = pl.program_id(0)
    phase = step // mp
    c = lax.rem(step, mp)
    me = me_ref[0]
    size = pieces[0].shape[0]
    width = heads * size
    own, model = block_out.shape

    @pl.when(step == 0)
    def _():
        for h in range(heads):
            for k in range(mp):
                source = lax.rem(me - k + mp, mp)
                row = pl.multiple_of(source * width + h * size, size)
                att[pl.ds(row, size)] = pieces[h * mp + k][...]
        _, inputs = embed_rows(ids[...], table[...])
        middle = inputs + nn(att[...].astype(f32).T.astype(bf16), w_out[...])
        normed, inverse = layer_stats(middle)
        xhat[...] = normed
        inv[...] = inverse
        mid = normed * gain[...] + bias[...]
        norm_mid[...] = mid.astype(bf16)
        norm_mid_t[...] = mid.T.astype(bf16)
        total[...] = middle + down_bias[...]

    @pl.when(phase == 0)
    def _():
        pre = nn(norm_mid[...], w_up[0]) + vec[c, 0:1]
        value, grad = gelu_parts(pre)
        value = value.astype(bf16)
        hidden[c] = value
        slope[c] = grad
        total[...] += nn(value, w_down[0])

    @pl.when(step == mp - 1)
    def _():
        low = total[...].astype(bf16)
        out_low[...] = low
        block_out[...] = low
        out_low_t[...] = low.astype(f32).T.astype(bf16)
        logit[...] = jnp.zeros_like(logit)

    @pl.when(phase == 1)
    def _():
        pre = nn(out_low[...], w_pred[0]) + vec[c, 1:2]
        value, grad = gelu_parts(pre)
        value = value.astype(bf16)
        p_hidden[c] = value
        p_slope[c] = grad
        logit[...] += jnp.sum(value.astype(f32) * vec[c, 2:3], axis=1, keepdims=True)

    @pl.when(step == 2 * mp - 1)
    def _():
        label_rows = jnp.broadcast_to(labels[0].astype(f32), (128, own)).T
        label = label_rows[:, :1]
        x = logit[...] + logit_bias[...]
        fall = jnp.exp(-jnp.abs(x))
        loss = jnp.maximum(x, 0.0) + jnp.log(1.0 + fall) - label * x
        grad = jnp.where(x >= 0, 1.0, fall) / (1.0 + fall) - label
        d_scalar[0:1] = jnp.broadcast_to(jnp.sum(loss, axis=0, keepdims=True), (1, 128))
        d_scalar[1:2] = jnp.broadcast_to(jnp.sum(grad, axis=0, keepdims=True), (1, 128))
        g_logit[...] = grad.astype(bf16).astype(f32)
        total[...] = cotangent[...].astype(f32)

    @pl.when(phase == 2)
    def _():
        g = g_logit[...]
        g_pre = g * vec[c, 2:3] * p_slope[c]
        d_vec[c, 1:2] = jnp.sum(g_pre, axis=0, keepdims=True)
        d_vec[c, 2:3] = jnp.sum(g * p_hidden[c].astype(f32), axis=0, keepdims=True)
        g_low = g_pre.astype(bf16)
        d_pred[0] = nn(out_low_t[...], g_low).astype(bf16)
        total[...] += nt(g_low, w_pred[0])

    @pl.when(step == 3 * mp - 1)
    def _():
        g_out = total[...]
        d_norm[2:3] = jnp.sum(g_out, axis=0, keepdims=True)
        grad_mid[...] = g_out
        out_low[...] = g_out.astype(bf16)
        total[...] = jnp.zeros_like(total)

    @pl.when(phase == 3)
    def _():
        g_low = out_low[...]
        d_down[0] = tn(hidden[c], g_low).astype(bf16)
        g_up = nt(g_low, w_down[0]) * slope[c]
        d_vec[c, 0:1] = jnp.sum(g_up, axis=0, keepdims=True)
        g_up = g_up.astype(bf16)
        d_up[0] = nn(norm_mid_t[...], g_up).astype(bf16)
        total[...] += nt(g_up, w_up[0])

    @pl.when(step == 4 * mp - 1)
    def _():
        g_norm = total[...]
        normed = xhat[...]
        d_norm[0:1] = jnp.sum(g_norm * normed, axis=0, keepdims=True)
        d_norm[1:2] = jnp.sum(g_norm, axis=0, keepdims=True)
        g_mid = grad_mid[...] + norm_back(g_norm, normed, inv[...], gain[...])
        grad_mid[...] = g_mid
        g_low = g_mid.astype(bf16)
        d_out[...] = nn(att[...], g_low).astype(bf16)
        att[...] = nt(w_out[...], g_low).astype(bf16)
        for h in range(heads):
            for k in range(mp):
                target = lax.rem(me + k, mp)
                row = pl.multiple_of(target * width + h * size, size)
                back[h * mp + k][...] = att[pl.ds(row, size)]


def rows_call(me, pieces, heads, ids, labels, cotangent, table, w_out, gain, bias, down_bias, logit_bias, vec, weights):
    mp = vec.shape[0]
    size, own = pieces[0].shape
    model = table.shape[1]
    hid = vec.shape[2]
    total_width = mp * heads * size
    (up, up_at), (down, down_at), (pred, pred_at) = weights

    def outer(row):
        return lambda s, m: (jnp.where((s // mp == 0) | (s // mp == 3), lax.rem(s, mp), mp - 1), row, 0)

    def inner(row):
        return lambda s, m: (
            jnp.where(s // mp == 0, 0, jnp.where(s // mp == 3, mp - 1, lax.rem(s, mp))),
            row,
            0,
        )

    def last(phase):
        return lambda s, m: (
            jnp.where(s // mp < phase, 0, jnp.where(s // mp == phase, lax.rem(s, mp), mp - 1)),
            0,
            0,
        )

    outs = [jax.ShapeDtypeStruct((size, own), bf16)] * len(pieces) + [
        jax.ShapeDtypeStruct((own, model), bf16),
        jax.ShapeDtypeStruct((own, model), f32),
        jax.ShapeDtypeStruct((mp, model, hid), bf16),
        jax.ShapeDtypeStruct((mp, hid, model), bf16),
        jax.ShapeDtypeStruct((mp, model, hid), bf16),
        jax.ShapeDtypeStruct((total_width, model), bf16),
        jax.ShapeDtypeStruct((mp, 3, hid), f32),
        jax.ShapeDtypeStruct((3, model), f32),
        jax.ShapeDtypeStruct((2, 128), f32),
    ]
    out_specs = [full(o.shape) for o in outs]
    base = len(pieces)
    out_specs[base + 2] = pl.BlockSpec((1, model, hid), last(3))
    out_specs[base + 3] = pl.BlockSpec((1, hid, model), last(3))
    out_specs[base + 4] = pl.BlockSpec((1, model, hid), last(2))
    ins = [*pieces, ids]
    tail = [cotangent, table, w_out, gain, bias, down_bias, logit_bias, vec]
    return pl.pallas_call(
        functools.partial(rows_kernel, mp, heads),
        grid_spec=pltpu.PrefetchScalarGridSpec(
            num_scalar_prefetch=1,
            grid=(4 * mp,),
            in_specs=[full(a.shape) for a in ins]
            + [pl.BlockSpec((1, 1, own), lambda s, m: (m[0], 0, 0))]
            + [full(a.shape) for a in tail]
            + [
                pl.BlockSpec((1, model, hid), outer(up_at)),
                pl.BlockSpec((1, hid, model), outer(down_at)),
                pl.BlockSpec((1, model, hid), inner(pred_at)),
            ],
            out_specs=out_specs,
            scratch_shapes=[
                pltpu.VMEM((total_width, own), bf16),
                pltpu.VMEM((own, model), f32),
                pltpu.VMEM((own, 1), f32),
                pltpu.VMEM((own, model), bf16),
                pltpu.VMEM((model, own), bf16),
                pltpu.VMEM((own, model), f32),
                pltpu.VMEM((own, model), bf16),
                pltpu.VMEM((model, own), bf16),
                pltpu.VMEM((mp, own, hid), bf16),
                pltpu.VMEM((mp, own, hid), f32),
                pltpu.VMEM((mp, own, hid), bf16),
                pltpu.VMEM((mp, own, hid), f32),
                pltpu.VMEM((own, 1), f32),
                pltpu.VMEM((own, 1), f32),
            ],
        ),
        out_shape=outs,
        compiler_params=params(),
        cost_estimate=pl.CostEstimate(
            flops=18 * own * model * hid * mp, bytes_accessed=20 << 20, transcendentals=2 * own * hid * mp
        ),
        name="rows",
    )(me, *ins, labels, *tail, up, down, pred)


def tail_kernel(mp, heads, me_ref, *refs):
    count = heads * mp
    pieces = refs[:count]
    w_joint, ids, table, gain, grad_mid, grad_in, d_embed, d_norm, parts = refs[count:]
    me = me_ref[0]
    third = pieces[0].shape[0]
    width = heads * third
    for h in range(heads):
        for k in range(mp):
            source = lax.rem(me - k + mp, mp)
            row = pl.multiple_of(source * width + h * third, third)
            parts[pl.ds(row, third)] = pieces[h * mp + k][...]
    g_norm = tn(parts[...], w_joint[...])
    one_hot_t, inputs = embed_rows(ids[...], table[...])
    normed, inverse = layer_stats(inputs)
    d_norm[0:1] = jnp.sum(g_norm * normed, axis=0, keepdims=True)
    d_norm[1:2] = jnp.sum(g_norm, axis=0, keepdims=True)
    g_in = grad_mid[...] + norm_back(g_norm, normed, inverse, gain[...])
    first = g_in.astype(bf16)
    grad_in[...] = first
    rest = g_in - first.astype(f32)
    second = rest.astype(bf16)
    third_part = (rest - second.astype(f32)).astype(bf16)
    hot = one_hot_t.astype(bf16)
    d_embed[...] = nn(hot, first) + nn(hot, second) + nn(hot, third_part)


def tail_call(me, pieces, heads, w_joint, ids, table, gain, grad_mid):
    mp = len(pieces) // heads
    own, model = grad_mid.shape
    outs = [
        jax.ShapeDtypeStruct((own, model), bf16),
        jax.ShapeDtypeStruct(table.shape, f32),
        jax.ShapeDtypeStruct((2, model), f32),
    ]
    ins = [*pieces, w_joint, ids, table, gain, grad_mid]
    return pl.pallas_call(
        functools.partial(tail_kernel, mp, heads),
        grid_spec=pltpu.PrefetchScalarGridSpec(
            num_scalar_prefetch=1,
            grid=(1,),
            in_specs=[full(a.shape) for a in ins],
            out_specs=[full(o.shape) for o in outs],
            scratch_shapes=[pltpu.VMEM(w_joint.shape, bf16) if w_joint.shape[1] == own else pltpu.VMEM((w_joint.shape[0], own), bf16)],
        ),
        out_shape=outs,
        compiler_params=params(),
        cost_estimate=pl.CostEstimate(flops=4 * own * model * model, bytes_accessed=6 << 20, transcendentals=0),
        name="tail",
    )(me, *ins)


def shift_pairs(count, k):
    return [(s, (s + k) % count) for s in range(count)]


def exchange(parts, axis, count):
    return [parts[0]] + [
        lax.ppermute(parts[k], axis, shift_pairs(count, k)) for k in range(1, count)
    ]


def swap(value, axis, count, bit):
    return lax.ppermute(value, axis, [(s, s ^ bit) for s in range(count)])


def sum_all(value, dp, mp):
    rows = value.shape[0]
    me_dp, me_mp = lax.axis_index("dp"), lax.axis_index("mp")
    bits = []
    bit = 1
    while bit < dp:
        bits.append(bit)
        bit *= 2
    current = value
    for bit in bits:
        half = current.shape[0] // 2
        mine = (me_dp // bit) % 2
        kept = lax.dynamic_slice_in_dim(current, mine * half, half, 0)
        sent = lax.dynamic_slice_in_dim(current, (1 - mine) * half, half, 0).astype(bf16)
        current = kept + swap(sent, "dp", dp, bit).astype(f32)
    piece = current.shape[0] // mp
    sent = [
        lax.dynamic_slice_in_dim(current, ((me_mp + k) % mp) * piece, piece, 0) for k in range(mp)
    ]
    got = exchange([sent[0]] + [s.astype(bf16) for s in sent[1:]], "mp", mp)
    low = sum(g.astype(f32) for g in got).astype(bf16)
    back = exchange([low] * mp, "mp", mp)
    current = jnp.zeros((piece * mp, value.shape[1]), bf16)
    for k in range(mp):
        current = lax.dynamic_update_slice_in_dim(
            current, back[k], ((me_mp - k) % mp) * piece, 0
        )
    for bit in reversed(bits):
        other = swap(current, "dp", dp, bit)
        mine = (me_dp // bit) % 2
        current = jnp.where(
            mine == 0,
            jnp.concatenate([current, other], axis=0),
            jnp.concatenate([other, current], axis=0),
        )
    return current.astype(f32)


def per_device(
    byte_ids,
    embed_table,
    boundary_labels,
    out_cotangent,
    norm_one_gain,
    norm_one_bias,
    w_query,
    w_key,
    w_value,
    w_position,
    content_bias,
    position_bias,
    w_out,
    norm_two_gain,
    norm_two_bias,
    w_up,
    up_bias,
    w_down,
    down_bias,
    w_pred,
    pred_bias,
    w_logit,
    logit_bias,
):
    dp, mp = lax.axis_size("dp"), lax.axis_size("mp")
    me_dp, me_mp = lax.axis_index("dp"), lax.axis_index("mp")
    own = byte_ids.shape[0]
    assert boundary_labels.shape[0] == LEN and own * mp == LEN
    model = embed_table.shape[1]
    heads, size = content_bias.shape
    width = heads * size
    hid = w_up.shape[1]
    scale = 1.0 / math.sqrt(size)
    me = me_mp.astype(jnp.int32).reshape(1)
    row = lambda v: v.astype(f32).reshape(1, -1)

    joint_t = (
        jnp.stack([w_query.T, w_key.T, w_value.T])
        .reshape(3, heads, size, model)
        .transpose(1, 0, 2, 3)
        .reshape(3 * width, model)
    )
    flat = jnp.concatenate([up_bias, pred_bias, w_logit]).reshape(-1)
    rows_used = 3 * hid + 4 * width
    unit = dp * 16
    total_rows = -(-(rows_used + -(-flat.shape[0] // model)) // unit) * unit
    flat = jnp.pad(flat, (0, (total_rows - rows_used) * model - flat.shape[0]))
    pack = jnp.concatenate(
        [
            w_up.reshape(hid, model),
            w_down,
            w_pred.reshape(hid, model),
            w_out,
            joint_t,
            flat.reshape(-1, model),
        ],
        axis=0,
    )
    share = total_rows // dp
    pack = lax.dynamic_slice_in_dim(pack, me_dp * share, share, 0)
    whole = lax.all_gather(pack, ("mp", "dp"), axis=0, tiled=True).reshape(mp, total_rows, model)

    def weight(index, shape):
        if shape == (hid, model):
            return whole, index
        return whole[:, index * hid : (index + 1) * hid].reshape(mp, *shape), 0

    weights = (weight(0, (model, hid)), weight(1, (hid, model)), weight(2, (model, hid)))
    out_whole = whole[:, 3 * hid : 3 * hid + width].reshape(mp * width, model)
    joint_whole = whole[:, 3 * hid + width : rows_used].reshape(mp * 3 * width, model)
    vec = whole[:, rows_used:].reshape(mp, -1)[:, : 3 * hid].reshape(mp, 3, hid).astype(f32)

    sin_np, cos_np = feature_tables(model)
    feature = np.concatenate([cos_np, sin_np], axis=1).astype(jnp.bfloat16)
    tables = (
        jnp.asarray(feature),
        jnp.asarray(np.ascontiguousarray(feature.T)),
        jnp.asarray(sin_np),
        jnp.asarray(cos_np),
    )
    tables_t = (
        jnp.asarray(np.ascontiguousarray(sin_np.T)),
        jnp.asarray(np.ascontiguousarray(cos_np.T)),
    )

    ids_own = byte_ids.reshape(1, own)
    id_parts = exchange([ids_own] * mp, "mp", mp)
    w_joint = jnp.concatenate([w_query, w_key, w_value], axis=1)
    norm_all, qcat, kcat, kcat_t, v, v_t, shift = pre_call(
        me,
        id_parts,
        embed_table,
        row(norm_one_gain),
        row(norm_one_bias),
        w_joint,
        w_position,
        row(content_bias),
        row(position_bias),
        tables,
        heads,
        scale,
    )
    saved, sent = [], []
    for h in range(heads):
        expon, full_t, inv, *parts = fwd_call(me, h, qcat, kcat, v_t, mp, own, size)
        saved.append((expon, full_t, inv))
        sent += exchange(parts, "mp", mp)

    result = rows_call(
        me,
        sent,
        heads,
        ids_own,
        boundary_labels.reshape(mp, 1, own),
        out_cotangent,
        embed_table,
        out_whole,
        row(norm_two_gain),
        row(norm_two_bias),
        row(down_bias),
        row(logit_bias),
        vec,
        weights,
    )
    back = result[: heads * mp]
    block_out, grad_mid, d_up, d_down, d_pred, d_out, d_vec, d_norm_two, d_scalar = result[heads * mp :]

    d_flat = jnp.pad(
        d_vec.reshape(mp, 3 * hid).astype(bf16),
        ((0, 0), (0, (total_rows - rows_used) * model - 3 * hid)),
    ).reshape(mp, -1, model)
    grads = jnp.concatenate(
        [
            d_up.reshape(mp, hid, model),
            d_down,
            d_pred.reshape(mp, hid, model),
            d_out.reshape(mp, width, model),
            d_flat,
        ],
        axis=1,
    )
    used = grads.shape[1]
    extra = -used % (dp * 8)
    grads = jnp.pad(grads, ((0, 0), (0, extra), (0, 0)))
    grads = grads.reshape(mp, dp, (used + extra) // dp, model)
    grads = lax.psum_scatter(grads, "dp", scatter_dimension=1, tiled=True)
    grads = lax.psum_scatter(grads, "mp", scatter_dimension=0, tiled=True)
    grads = lax.all_gather(grads.reshape(-1, model), "dp", axis=0, tiled=True).astype(f32)

    arrived, d_joint, d_pos, d_cb, d_pb = [], [], 0.0, [], []
    for h in range(heads):
        pieces = exchange(back[h * mp : (h + 1) * mp], "mp", mp)
        parts = bwd_call(
            me,
            h,
            heads,
            pieces,
            *saved[h],
            qcat,
            kcat_t,
            v,
            shift,
            w_position,
            tables_t,
            norm_all,
            scale,
        )
        arrived += exchange(parts[:mp], "mp", mp)
        dw, dp_, dc, db = parts[mp:]
        d_joint.append(dw)
        lane = jnp.arange(width)[None, :]
        d_pos = d_pos + jnp.where((lane >= h * size) & (lane < (h + 1) * size), dp_, 0.0)
        d_cb.append(dc)
        d_pb.append(db)
    grad_input, d_embed, d_norm_one = tail_call(
        me, arrived, heads, joint_whole, ids_own, embed_table, row(norm_one_gain), grad_mid
    )

    bias_rows = jnp.concatenate(
        [jnp.concatenate(d_cb, axis=0), jnp.concatenate(d_pb, axis=0)], axis=0
    ).reshape(-1)
    bias_rows = jnp.pad(bias_rows, (0, 8 * model - bias_rows.shape[0])).reshape(8, model)
    by_seq = jnp.concatenate(
        [*d_joint, d_pos.reshape(-1, model).astype(bf16), bias_rows.astype(bf16)], axis=0
    )
    by_seq = lax.psum(by_seq, "dp").astype(f32)
    joint = by_seq[: 3 * width].reshape(heads, 3, size, model).transpose(1, 0, 2, 3)
    joint = joint.reshape(3, width, model).transpose(0, 2, 1)
    sum_pos = by_seq[3 * width : 4 * width].reshape(model, width)
    sum_bias = by_seq[4 * width :].reshape(-1)
    sum_cb = sum_bias[:width].reshape(heads, size)
    sum_pb = sum_bias[width : 2 * width].reshape(heads, size)

    scalars = lax.psum(d_scalar, ("dp", "mp"))
    vocab = embed_table.shape[0]
    small = jnp.concatenate([d_norm_one, d_norm_two], axis=0)
    pad_rows = -(vocab + 5) % (dp * mp * 8)
    sums = sum_all(
        jnp.concatenate([d_embed, small, jnp.zeros((pad_rows, model), f32)], axis=0), dp, mp
    )
    vec_sum = grads[3 * hid + width : used].reshape(-1)
    return (
        block_out,
        scalars[0, :1] / (LEN * dp),
        grad_input,
        sums[:vocab],
        sums[vocab],
        sums[vocab + 1],
        joint[0],
        joint[1],
        joint[2],
        sum_pos,
        sum_cb,
        sum_pb,
        grads[3 * hid : 3 * hid + width],
        sums[vocab + 2],
        sums[vocab + 3],
        grads[:hid].reshape(model, hid),
        vec_sum[:hid],
        grads[hid : 2 * hid],
        sums[vocab + 4],
        grads[2 * hid : 3 * hid].reshape(model, hid),
        vec_sum[hid : 2 * hid],
        vec_sum[2 * hid : 3 * hid],
        scalars[1, :1],
    )


def solution(mesh):
    by_rows = P(("dp", "mp"), None)
    columns = P(None, "mp")
    shard = P("mp", None)
    placed = (
        P(("dp", "mp")),
        P(),
        P("dp"),
        by_rows,
        P(),
        P(),
        columns,
        columns,
        columns,
        columns,
        shard,
        shard,
        shard,
        P(),
        P(),
        columns,
        P("mp"),
        shard,
        P(),
        columns,
        P("mp"),
        P("mp"),
        P(),
    )
    results = (
        by_rows,
        P(),
        by_rows,
        P(),
        P(),
        P(),
        columns,
        columns,
        columns,
        columns,
        shard,
        shard,
        shard,
        P(),
        P(),
        columns,
        P("mp"),
        shard,
        P(),
        columns,
        P("mp"),
        P("mp"),
        P(),
    )
    return jax.shard_map(
        per_device, mesh=mesh, in_specs=placed, out_specs=results, check_vma=False
    )
```

time: 841 us -> 495 us (0.59)
  waiting for transfers between devices: 504 us -> 202 us
  matrix products: 133 us -> 0 us
  Pallas kernels: 0 us -> 114 us
  other arithmetic: 73.4 us -> 12.5 us
  starting transfers between devices: 9.73 us -> 54.7 us
  blocking collectives: 64.3 us -> 39.8 us
  local copies, waits for them, and re-layouts: 29.1 us -> 45.8 us
    psum x6 -> x1, waiting for transfers between devices: 439 us -> 119 us  [per_device(): by_seq = lax.psum(by_seq, 'dp').astype(f32)]
    dot_general x54 -> x0, matrix products: 133 us -> none  [the longest x4 14.4 us: block_scores(): jnp.einsum('sqhm,km->shqk', posq_seq[:, row_low:row_high], key_feature[:r...]
    pallas_call x0 -> x7, Pallas kernels: none -> 114 us  [the longest x2 37 us: bwd_call(): pl.pallas_call(functools.partial(bwd_kernel, mp, own, head, heads, scale)...]
    ppermute x0 -> x33, waiting for transfers between devices: none -> 56.5 us  [the longest x27 42.2 us: exchange(): lax.ppermute(parts[k], axis, shift_pairs(count, k))]
    ppermute x0 -> x33, starting transfers between devices: none -> 54.5 us  [the longest x27 47.9 us: exchange(): lax.ppermute(parts[k], axis, shift_pairs(count, k))]
    reduce_scatter x1, waiting for transfers between devices: 36.1 us -> 0.02 us  [per_device(): grads = lax.psum_scatter(grads, 'mp', scatter_dimension=0, tiled=True)]
    psum x3 -> x1, blocking collectives: 64.3 us -> 39.8 us  [per_device(): scalars = lax.psum(d_scalar, ('dp', 'mp'))]
    convert_element_type x29 -> x3, other arithmetic: 24.8 us -> 3.2 us  [the longest x1 2.01 us: per_device(): lax.all_gather(grads.reshape(-1, model), 'dp', axis=0, tiled=True)]
  transfers between devices with their start and end apart: 8 -> 37, of which waited for: 8 -> 16; matrix products, arithmetic and copies ran while one was open for 7% -> 6% of each run, Pallas kernels for 0% -> 13%
where the time goes in v1:
time: 495 us; the launch traced here: 487 us
  waiting for transfers between devices  202 us (41%)
  Pallas kernels  114 us (23%)
  starting transfers between devices  54.7 us (11%)
  local copies, waits for them, and re-layouts  45.8 us (9%)
  blocking collectives  39.8 us (8%)
  between operations  17.7 us (4%)
  other arithmetic  12.5 us (3%)
    psum x1, waiting for transfers between devices, per_device(): by_seq = lax.psum(by_seq, 'dp').astype(f32)  119 us
    ppermute x27, starting transfers between devices, exchange(): lax.ppermute(parts[k], axis, shift_pairs(count, k))  47.9 us
    ppermute x27, waiting for transfers between devices, exchange(): lax.ppermute(parts[k], axis, shift_pairs(count, k))  42.2 us
    psum x1, blocking collectives, per_device(): scalars = lax.psum(d_scalar, ('dp', 'mp'))  39.8 us
    pallas_call x2, Pallas kernels, bwd_call(): pl.pallas_call(functools.partial(bwd_kernel, mp, own, head, heads, scale)...  37 us
    pallas_call x1, Pallas kernels, rows_call(): pl.pallas_call(functools.partial(rows_kernel, mp, heads), grid_spec=pltpu...  30.6 us
    unnamed x140, local copies, waits for them, and re-layouts  29.7 us
    pallas_call x2, Pallas kernels, fwd_call(): pl.pallas_call(functools.partial(fwd_kernel, mp, own), grid_spec=pltpu.Pr...  27.4 us
  transfers between devices with their start and end apart: 37, of which 16 were waited for; matrix products, arithmetic and copies ran while one was open for 6% of the time, Pallas kernels for 13%

profile of v1, /device:TPU:0, one launch (start us, length us, event | category | flops | bytes accessed | tf_op | source)
XLA Modules:
  0.0 486.8 jit_solution(17131704287586424860)
XLA Ops:
  18.3 3.1 collective-permute-start
  21.4 2.6 collective-permute-start.1
  33.1 13.2 %project.1 = (bf16[2048,512]{1,0:T(8,128)(2,1)}, bf16[2,2048,640]{2,1,0:T(8,128)(2,1)}, bf16[2048,640]{1,0:T(8,128)(2,1)}, bf16[640,2048]{1,0:T(8,128)(2,1)}, bf...) custom-call(s32[1]{0:T(128)} %bitcast.6.me_ref, s32[1,512]{1,0:T(1,128)} %bitcast.100, ...), custom_call_target="tpu_custom_call" | custom-call | flops 1610612736 | bytes 25165824 | tf_op jit(solution)/shard_map/project/pallas_call | solution.py:156
  46.3 13.8 %attend.2 = (bf16[8,2048,256]{2,1,0:T(8,128)(2,1)}, f32[64,2048]{1,0:T(8,128)}, f32[1,2048]{1,0:T(1,128)}, bf16[64,512]{1,0:T(8,128)(2,1)}, bf16[64,512]{1,0:T(8...) custom-call(s32[1]{0:T(128)} %bitcast.6.me_ref, bf16[2,2048,640]{2,1,0:T(8,128)(2,1)} %get-tuple-element.80.qcat.refs_7_, ...), custom_call_target="tpu_custom_call" | custom-call | flops 3543347968 | bytes 16777216 | tf_op jit(solution)/shard_map/attend/pallas_call | solution.py:237
  60.9 13.6 %attend.3 = (bf16[8,2048,256]{2,1,0:T(8,128)(2,1)}, f32[64,2048]{1,0:T(8,128)}, f32[1,2048]{1,0:T(1,128)}, bf16[64,512]{1,0:T(8,128)(2,1)}, bf16[64,512]{1,0:T(8...) custom-call(s32[1]{0:T(128)} %bitcast.6.me_ref, bf16[2,2048,640]{2,1,0:T(8,128)(2,1)} %get-tuple-element.80.qcat.refs_7_, ...), custom_call_target="tpu_custom_call" | custom-call | flops 3543347968 | bytes 16777216 | tf_op jit(solution)/shard_map/attend/pallas_call | solution.py:237
  75.0 3.0 collective-permute-start.5
  80.0 3.3 collective-permute-start.8
  83.3 26.5 %all-gather.4.cloned.1.call-done = bf16[8704,512]{1,0:T(8,128)(2,1)} async-done(((bf16[272,512]{1,0:T(8,128)(2,1)}), bf16[8704,512]{1,0:T(8,128)(2,1)}) %all-gather.4.cloned.1.call-update) | async-done | bytes 8912912 | tf_op jit(solution)/shard_map/all_gather | solution.py:778
  113.6 30.6 %rows.1 = (bf16[64,512]{1,0:T(8,128)(2,1)}, bf16[64,512]{1,0:T(8,128)(2,1)}, bf16[64,512]{1,0:T(8,128)(2,1)}, bf16[64,512]{1,0:T(8,128)(2,1)}, bf16[64,512]{1,0:...) custom-call(s32[1]{0:T(128)} %bitcast.6.me_ref, ...), custom_call_target="tpu_custom_call" | custom-call | flops 9663676416 | bytes 20971520 | tf_op jit(solution)/shard_map/rows/pallas_call | solution.py:573
  146.0 2.7 collective-permute-start.15
  148.7 2.4 collective-permute-start.17
  151.1 3.1 constant_dynamic-update-slice_fusion.9
  162.8 18.3 %attend_back.3 = (bf16[192,512]{1,0:T(8,128)(2,1)}, bf16[192,512]{1,0:T(8,128)(2,1)}, bf16[192,512]{1,0:T(8,128)(2,1)}, bf16[192,512]{1,0:T(8,128)(2,1)}, bf16[1...) custom-call(s32[1]{0:T(128)} %bitcast.6.me_ref, ...), custom_call_target="tpu_custom_call" | custom-call | flops 5153960960 | bytes 25165824 | tf_op jit(solution)/shard_map/attend_back/pallas_call | solution.py:365
  182.7 18.7 %attend_back.2 = (bf16[192,512]{1,0:T(8,128)(2,1)}, bf16[192,512]{1,0:T(8,128)(2,1)}, bf16[192,512]{1,0:T(8,128)(2,1)}, bf16[192,512]{1,0:T(8,128)(2,1)}, bf16[1...) custom-call(s32[1]{0:T(128)} %bitcast.6.me_ref, ...), custom_call_target="tpu_custom_call" | custom-call | flops 5153960960 | bytes 25165824 | tf_op jit(solution)/shard_map/attend_back/pallas_call | solution.py:365
  207.4 119.4 %all-reduce.7.cloned.1.call-done = (bf16[520,512]{1,0:T(8,128)(2,1)}, bf16[4,8,224,512]{3,2,1,0:T(8,128)(2,1)}) async-done(((bf16[520,512]{1,0:T(8,128)(2,1)}, bf16[4,8,224,512]{3,2,1,0:T(8,128)(2,1)}), (bf16[520,512]{1,0:T(8,128)(2,1)}, bf16[4,8,224,512]{3,2,1,0:T(8,128)(2,1)})) %all-reduce.7.cloned.1.call-update) | async-done | bytes 7872528 | tf_op jit(solution)/shard_map/psum | solution.py:903
  326.8 2.8 constant_dynamic-slice_fusion.1
  331.2 2.4 collective-permute-start.13
  336.2 3.3 collective-permute-done.12.refs_1_
  339.5 4.5 collective-permute-start.20
  344.1 2.7 slice.147
  346.7 10.0 %collective-permute-done.13.refs_2_ = bf16[192,512]{1,0:T(8,128)(2,1)S(1)} collective-permute-done((bf16[192,512]{1,0:T(8,128)(2,1)S(1)}, bf16[192,512]{1,0:T(8,128)(2,1)S(1)}, u32[]{:S(2)}, u32[]{:S(2)}) %collective-permute-start.13) | collective-permute-done | bytes 196640 | tf_op jit(solution)/shard_map/ppermute | solution.py:671
  356.7 7.8 %collective-permute-done.18.refs_5_ = bf16[192,512]{1,0:T(8,128)(2,1)S(1)} collective-permute-done((bf16[192,512]{1,0:T(8,128)(2,1)S(1)}, bf16[192,512]{1,0:T(8,128)(2,1)S(1)}, u32[]{:S(2)}, u32[]{:S(2)}) %collective-permute-start.18) | collective-permute-done | bytes 196640 | tf_op jit(solution)/shard_map/ppermute | solution.py:671
  364.5 13.6 %collective-permute-done.19.refs_6_ = bf16[192,512]{1,0:T(8,128)(2,1)S(1)} collective-permute-done((bf16[192,512]{1,0:T(8,128)(2,1)S(1)}, bf16[192,512]{1,0:T(8,128)(2,1)S(1)}, u32[]{:S(2)}, u32[]{:S(2)}) %collective-permute-start.19) | collective-permute-done | bytes 196640 | tf_op jit(solution)/shard_map/ppermute | solution.py:671
  378.9 5.6 %tail.1 = (bf16[512,512]{1,0:T(8,128)(2,1)}, f32[256,512]{1,0:T(8,128)}, f32[2,512]{1,0:T(2,128)}) custom-call(s32[1]{0:T(128)} %bitcast.6.me_ref, bf16[192,512]{1,0:T(8,128)(2,1)} %get-tuple-element.104.refs_0_, bf16[192,512]{1,0:T(8,128)(2,1)} %copy-done.11, bf16[192,512]{1,0:T(8,128)(2,1)} %copy-done.12, bf16[192,512]{1,0:T(8,128)(2,1)} %copy-done.13, ...), custom_call_target="tpu_custom_call" | custom-call | flops 536870912 | bytes 6291456 | tf_op jit(solution)/shard_map/tail/pallas_call | solution.py:649
  389.2 3.9 collective-permute-done.22
  394.7 2.8 collective-permute-done.23
  397.5 6.9 %collective-permute-start.26 = (bf16[16,512]{1,0:T(8,128)(2,1)S(1)}, bf16[16,512]{1,0:T(8,128)(2,1)S(1)}, u32[]{:S(2)}, u32[]{:S(2)}) collective-permute-start(bf16[16,512]{1,0:T(8,128)(2,1)S(1)} %get-tuple-element.227), channel_id=1, source_target_pairs={{0,3},{1,0},{2,1},{3,2},{4,7},{5,4},{6,5},{7,6},{8,11},{9,8},{10,9... | collective-permute-start | bytes 49160 | tf_op jit(solution)/shard_map/ppermute | solution.py:671
  405.8 3.2 collective-permute-done.25
  411.3 3.0 collective-permute-start.29
  418.0 2.8 collective-permute-done.30
  422.5 3.3 collective-permute-done.31
  426.0 39.8 %psum.14 = f32[2,128]{1,0:T(2,128)S(1)} all-reduce(f32[2,128]{1,0:T(2,128)S(1)} %copy-done.40), channel_id=1, replica_groups=mesh['dp'=8,'mp'=4] {'dp','mp'}, use_global_device_ids=true, to_apply=%region_0.1 | all-reduce | flops 256 | bytes 2048 | tf_op jit(solution)/shard_map/psum | solution.py:911
  (263 shorter events, 76.5 us)
Async XLA Ops:
  7.2 102.5 %all-gather.4.cloned.1.call-start = ((), (), s32[]{:S(2)}) async-start(), calls=%async_computation.1 | async-start | bytes 9191424 | tf_op jit(solution)/shard_map/all_gather | solution.py:778
  18.2 308.6 %all-reduce.7.cloned.1.call-start = ((), (), s32[]{:S(2)}) async-start(), calls=%async_computation.4 | async-start | bytes 15745024 | tf_op jit(solution)/shard_map/psum | solution.py:903
  18.3 14.2 %collective-permute-start = (s32[1,512]{1,0:T(1,128)S(1)}, s32[1,512]{1,0:T(1,128)S(1)}, u32[]{:S(2)}, u32[]{:S(2)}) collective-permute-start(s32[1,512]{1,0:T(1,128)S(1)} %bitcast.103), channel_id=1, source_target_pairs={{0,1},{1,2},{2,3},{3,0},{4,5},{5,6},{6,7},{7,4},{8,9},{9,10},{10,1... | collective-permute-start | bytes 6152 | tf_op jit(solution)/shard_map/ppermute | solution.py:671
  21.4 11.1 %collective-permute-start.1 = (s32[1,512]{1,0:T(1,128)S(1)}, s32[1,512]{1,0:T(1,128)S(1)}, u32[]{:S(2)}, u32[]{:S(2)}) collective-permute-start(s32[1,512]{1,0:T(1,128)S(1)} %bitcast.104), channel_id=1, source_target_pairs={{0,2},{1,3},{2,0},{3,1},{4,6},{5,7},{6,4},{7,5},{8,10},{9,11},{10,... | collective-permute-start | bytes 6152 | tf_op jit(solution)/shard_map/ppermute | solution.py:671
  24.0 8.5 %collective-permute-start.2 = (s32[1,512]{1,0:T(1,128)S(1)}, s32[1,512]{1,0:T(1,128)S(1)}, u32[]{:S(2)}, u32[]{:S(2)}) collective-permute-start(s32[1,512]{1,0:T(1,128)S(1)} %bitcast.105), channel_id=1, source_target_pairs={{0,3},{1,0},{2,1},{3,2},{4,7},{5,4},{6,5},{7,6},{8,11},{9,8},{10,9... | collective-permute-start | bytes 6152 | tf_op jit(solution)/shard_map/ppermute | solution.py:671
  60.1 19.9 %collective-permute-start.3 = (bf16[64,512]{1,0:T(8,128)(2,1)}, bf16[64,512]{1,0:T(8,128)(2,1)S(1)}, u32[]{:S(2)}, u32[]{:S(2)}) collective-permute-start(bf16[64,512]{1,0:T(8,128)(2,1)} %get-tuple-element.84), channel_id=1, source_target_pairs={{0,1},{1,2},{2,3},{3,0},{4,5},{5,6},{6,7},{7,4},{8,9},{9,10},{10,1... | collective-permute-start | bytes 196616 | tf_op jit(solution)/shard_map/ppermute | solution.py:671
  74.5 38.4 %collective-permute-start.4 = (bf16[64,512]{1,0:T(8,128)(2,1)S(1)}, bf16[64,512]{1,0:T(8,128)(2,1)S(1)}, u32[]{:S(2)}, u32[]{:S(2)}) collective-permute-start(bf16[64,512]{1,0:T(8,128)(2,1)S(1)} %copy-done.55), channel_id=1, source_target_pairs={{0,2},{1,3},{2,0},{3,1},{4,6},{5,7},{6,4},{7,5},{8,10},{9,11},{10,... | collective-permute-start | bytes 196616 | tf_op jit(solution)/shard_map/ppermute | solution.py:671
  75.0 37.9 %collective-permute-start.5 = (bf16[64,512]{1,0:T(8,128)(2,1)S(1)}, bf16[64,512]{1,0:T(8,128)(2,1)S(1)}, u32[]{:S(2)}, u32[]{:S(2)}) collective-permute-start(bf16[64,512]{1,0:T(8,128)(2,1)S(1)} %copy-done.54), channel_id=1, source_target_pairs={{0,3},{1,0},{2,1},{3,2},{4,7},{5,4},{6,5},{7,6},{8,11},{9,8},{10,9... | collective-permute-start | bytes 196616 | tf_op jit(solution)/shard_map/ppermute | solution.py:671
  78.0 34.9 %collective-permute-start.6 = (bf16[64,512]{1,0:T(8,128)(2,1)}, bf16[64,512]{1,0:T(8,128)(2,1)S(1)}, u32[]{:S(2)}, u32[]{:S(2)}) collective-permute-start(bf16[64,512]{1,0:T(8,128)(2,1)} %get-tuple-element.88), channel_id=1, source_target_pairs={{0,1},{1,2},{2,3},{3,0},{4,5},{5,6},{6,7},{7,4},{8,9},{9,10},{10,1... | collective-permute-start | bytes 196616 | tf_op jit(solution)/shard_map/ppermute | solution.py:671
  78.5 34.4 %collective-permute-start.7 = (bf16[64,512]{1,0:T(8,128)(2,1)}, bf16[64,512]{1,0:T(8,128)(2,1)S(1)}, u32[]{:S(2)}, u32[]{:S(2)}) collective-permute-start(bf16[64,512]{1,0:T(8,128)(2,1)} %get-tuple-element.89), channel_id=1, source_target_pairs={{0,2},{1,3},{2,0},{3,1},{4,6},{5,7},{6,4},{7,5},{8,10},{9,11},{10,... | collective-permute-start | bytes 196616 | tf_op jit(solution)/shard_map/ppermute | solution.py:671
  80.0 33.0 %collective-permute-start.8 = (bf16[64,512]{1,0:T(8,128)(2,1)}, bf16[64,512]{1,0:T(8,128)(2,1)S(1)}, u32[]{:S(2)}, u32[]{:S(2)}) collective-permute-start(bf16[64,512]{1,0:T(8,128)(2,1)} %get-tuple-element.90), channel_id=1, source_target_pairs={{0,3},{1,0},{2,1},{3,2},{4,7},{5,4},{6,5},{7,6},{8,11},{9,8},{10,9... | collective-permute-start | bytes 196616 | tf_op jit(solution)/shard_map/ppermute | solution.py:671
  144.3 37.7 %collective-permute-start.9 = (bf16[64,512]{1,0:T(8,128)(2,1)}, bf16[64,512]{1,0:T(8,128)(2,1)S(1)}, u32[]{:S(2)}, u32[]{:S(2)}) collective-permute-start(bf16[64,512]{1,0:T(8,128)(2,1)} %get-tuple-element.94), channel_id=1, source_target_pairs={{0,1},{1,2},{2,3},{3,0},{4,5},{5,6},{6,7},{7,4},{8,9},{9,10},{10,1... | collective-permute-start | bytes 196616 | tf_op jit(solution)/shard_map/ppermute | solution.py:671
  144.3 37.7 %collective-permute-start.10 = (bf16[64,512]{1,0:T(8,128)(2,1)}, bf16[64,512]{1,0:T(8,128)(2,1)S(1)}, u32[]{:S(2)}, u32[]{:S(2)}) collective-permute-start(bf16[64,512]{1,0:T(8,128)(2,1)} %get-tuple-element.95), channel_id=1, source_target_pairs={{0,2},{1,3},{2,0},{3,1},{4,6},{5,7},{6,4},{7,5},{8,10},{9,11},{10,... | collective-permute-start | bytes 196616 | tf_op jit(solution)/shard_map/ppermute | solution.py:671
  146.0 13.9 %collective-permute-start.15 = (bf16[64,512]{1,0:T(8,128)(2,1)}, bf16[64,512]{1,0:T(8,128)(2,1)S(1)}, u32[]{:S(2)}, u32[]{:S(2)}) collective-permute-start(bf16[64,512]{1,0:T(8,128)(2,1)} %get-tuple-element.109), channel_id=1, source_target_pairs={{0,1},{1,2},{2,3},{3,0},{4,5},{5,6},{6,7},{7,4},{8,9},{9,10},{10,1... | collective-permute-start | bytes 196616 | tf_op jit(solution)/shard_map/ppermute | solution.py:671
  148.7 13.5 %collective-permute-start.16 = (bf16[64,512]{1,0:T(8,128)(2,1)}, bf16[64,512]{1,0:T(8,128)(2,1)S(1)}, u32[]{:S(2)}, u32[]{:S(2)}) collective-permute-start(bf16[64,512]{1,0:T(8,128)(2,1)} %get-tuple-element.110), channel_id=1, source_target_pairs={{0,2},{1,3},{2,0},{3,1},{4,6},{5,7},{6,4},{7,5},{8,10},{9,11},{10,... | collective-permute-start | bytes 196616 | tf_op jit(solution)/shard_map/ppermute | solution.py:671
  148.7 13.5 %collective-permute-start.17 = (bf16[64,512]{1,0:T(8,128)(2,1)}, bf16[64,512]{1,0:T(8,128)(2,1)S(1)}, u32[]{:S(2)}, u32[]{:S(2)}) collective-permute-start(bf16[64,512]{1,0:T(8,128)(2,1)} %get-tuple-element.111), channel_id=1, source_target_pairs={{0,3},{1,0},{2,1},{3,2},{4,7},{5,4},{6,5},{7,6},{8,11},{9,8},{10,9... | collective-permute-start | bytes 196616 | tf_op jit(solution)/shard_map/ppermute | solution.py:671
  159.9 22.1 %collective-permute-start.11 = (bf16[64,512]{1,0:T(8,128)(2,1)S(1)}, bf16[64,512]{1,0:T(8,128)(2,1)S(1)}, u32[]{:S(2)}, u32[]{:S(2)}) collective-permute-start(bf16[64,512]{1,0:T(8,128)(2,1)S(1)} %copy-done.47), channel_id=1, source_target_pairs={{0,3},{1,0},{2,1},{3,2},{4,7},{5,4},{6,5},{7,6},{8,11},{9,8},{10,9... | collective-permute-start | bytes 196616 | tf_op jit(solution)/shard_map/ppermute | solution.py:671
  206.2 179.6 %reduce-scatter.5.cloned.1.call-start = ((), (), s32[]{:S(2)}) async-start(), calls=%async_computation.2 | async-start | bytes 1146880 | tf_op jit(solution)/shard_map/reduce_scatter | solution.py:864
  329.6 143.1 %all-gather.6.cloned.1.call-start = ((), (), s32[]{:S(2)}) async-start(), calls=%async_computation.3 | async-start | bytes 2064384 | tf_op jit(solution)/shard_map/all_gather | solution.py:865
  329.7 9.8 %collective-permute-start.12 = (bf16[192,512]{1,0:T(8,128)(2,1)S(1)}, bf16[192,512]{1,0:T(8,128)(2,1)S(1)}, u32[]{:S(2)}, u32[]{:S(2)}) collective-permute-start(bf16[192,512]{1,0:T(8,128)(2,1)S(1)} %copy-done.46), channel_id=1, source_target_pairs={{0,1},{1,2},{2,3},{3,0},{4,5},{5,6},{6,7},{7,4},{8,9},{9,10},{10,1... | collective-permute-start | bytes 589832 | tf_op jit(solution)/shard_map/ppermute | solution.py:671
  331.2 25.5 %collective-permute-start.13 = (bf16[192,512]{1,0:T(8,128)(2,1)S(1)}, bf16[192,512]{1,0:T(8,128)(2,1)S(1)}, u32[]{:S(2)}, u32[]{:S(2)}) collective-permute-start(bf16[192,512]{1,0:T(8,128)(2,1)S(1)} %copy-done.45), channel_id=1, source_target_pairs={{0,2},{1,3},{2,0},{3,1},{4,6},{5,7},{6,4},{7,5},{8,10},{9,11},{10,... | collective-permute-start | bytes 589832 | tf_op jit(solution)/shard_map/ppermute | solution.py:671
  333.7 23.1 %collective-permute-start.14 = (bf16[192,512]{1,0:T(8,128)(2,1)S(1)}, bf16[192,512]{1,0:T(8,128)(2,1)S(1)}, u32[]{:S(2)}, u32[]{:S(2)}) collective-permute-start(bf16[192,512]{1,0:T(8,128)(2,1)S(1)} %copy-done.44), channel_id=1, source_target_pairs={{0,3},{1,0},{2,1},{3,2},{4,7},{5,4},{6,5},{7,6},{8,11},{9,8},{10,9... | collective-permute-start | bytes 589832 | tf_op jit(solution)/shard_map/ppermute | solution.py:671
  335.1 29.4 %collective-permute-start.18 = (bf16[192,512]{1,0:T(8,128)(2,1)S(1)}, bf16[192,512]{1,0:T(8,128)(2,1)S(1)}, u32[]{:S(2)}, u32[]{:S(2)}) collective-permute-start(bf16[192,512]{1,0:T(8,128)(2,1)S(1)} %copy-done.43), channel_id=1, source_target_pairs={{0,1},{1,2},{2,3},{3,0},{4,5},{5,6},{6,7},{7,4},{8,9},{9,10},{10,1... | collective-permute-start | bytes 589832 | tf_op jit(solution)/shard_map/ppermute | solution.py:671
  335.7 42.4 %collective-permute-start.19 = (bf16[192,512]{1,0:T(8,128)(2,1)S(1)}, bf16[192,512]{1,0:T(8,128)(2,1)S(1)}, u32[]{:S(2)}, u32[]{:S(2)}) collective-permute-start(bf16[192,512]{1,0:T(8,128)(2,1)S(1)} %copy-done.42), channel_id=1, source_target_pairs={{0,2},{1,3},{2,0},{3,1},{4,6},{5,7},{6,4},{7,5},{8,10},{9,11},{10,... | collective-permute-start | bytes 589832 | tf_op jit(solution)/shard_map/ppermute | solution.py:671
  339.5 38.6 %collective-permute-start.20 = (bf16[192,512]{1,0:T(8,128)(2,1)S(1)}, bf16[192,512]{1,0:T(8,128)(2,1)S(1)}, u32[]{:S(2)}, u32[]{:S(2)}) collective-permute-start(bf16[192,512]{1,0:T(8,128)(2,1)S(1)} %copy-done.41), channel_id=1, source_target_pairs={{0,3},{1,0},{2,1},{3,2},{4,7},{5,4},{6,5},{7,6},{8,11},{9,8},{10,9... | collective-permute-start | bytes 589832 | tf_op jit(solution)/shard_map/ppermute | solution.py:671
  387.5 5.6 %collective-permute-start.22 = (bf16[128,512]{1,0:T(8,128)(2,1)S(1)}, bf16[128,512]{1,0:T(8,128)(2,1)S(1)}, u32[]{:S(2)}, u32[]{:S(2)}) collective-permute-start(bf16[128,512]{1,0:T(8,128)(2,1)S(1)} %dynamic-slice_convert_fusion.1), channel_id=1, source_target_pairs={{0,8},{4,12},{8,0},{12,4},{16,24},{20,28},{24,16},{28,20},{1,9},{5... | collective-permute-start | bytes 393224 | tf_op jit(solution)/shard_map/ppermute | solution.py:676
  397.5 8.3 %collective-permute-start.26 = (bf16[16,512]{1,0:T(8,128)(2,1)S(1)}, bf16[16,512]{1,0:T(8,128)(2,1)S(1)}, u32[]{:S(2)}, u32[]{:S(2)}) collective-permute-start(bf16[16,512]{1,0:T(8,128)(2,1)S(1)} %get-tuple-element.227), channel_id=1, source_target_pairs={{0,3},{1,0},{2,1},{3,2},{4,7},{5,4},{6,5},{7,6},{8,11},{9,8},{10,9... | collective-permute-start | bytes 49160 | tf_op jit(solution)/shard_map/ppermute | solution.py:671
  404.8 5.6 %collective-permute-start.24 = (bf16[16,512]{1,0:T(8,128)(2,1)S(1)}, bf16[16,512]{1,0:T(8,128)(2,1)S(1)}, u32[]{:S(2)}, u32[]{:S(2)}) collective-permute-start(bf16[16,512]{1,0:T(8,128)(2,1)S(1)} %get-tuple-element.226), channel_id=1, source_target_pairs={{0,1},{1,2},{2,3},{3,0},{4,5},{5,6},{6,7},{7,4},{8,9},{9,10},{10,1... | collective-permute-start | bytes 49160 | tf_op jit(solution)/shard_map/ppermute | solution.py:671
  410.4 5.6 %collective-permute-start.27 = (bf16[16,512]{1,0:T(8,128)(2,1)S(1)}, bf16[16,512]{1,0:T(8,128)(2,1)S(1)}, u32[]{:S(2)}, u32[]{:S(2)}) collective-permute-start(bf16[16,512]{1,0:T(8,128)(2,1)S(1)} %get-tuple-element.209), channel_id=1, source_target_pairs={{0,1},{1,2},{2,3},{3,0},{4,5},{5,6},{6,7},{7,4},{8,9},{9,10},{10,1... | collective-permute-start | bytes 49160 | tf_op jit(solution)/shard_map/ppermute | solution.py:671
  410.5 5.5 %collective-permute-start.28 = (bf16[16,512]{1,0:T(8,128)(2,1)S(1)}, bf16[16,512]{1,0:T(8,128)(2,1)S(1)}, u32[]{:S(2)}, u32[]{:S(2)}) collective-permute-start(bf16[16,512]{1,0:T(8,128)(2,1)S(1)} %get-tuple-element.209), channel_id=1, source_target_pairs={{0,2},{1,3},{2,0},{3,1},{4,6},{5,7},{6,4},{7,5},{8,10},{9,11},{10,... | collective-permute-start | bytes 49160 | tf_op jit(solution)/shard_map/ppermute | solution.py:671
  411.3 5.2 %collective-permute-start.29 = (bf16[16,512]{1,0:T(8,128)(2,1)S(1)}, bf16[16,512]{1,0:T(8,128)(2,1)S(1)}, u32[]{:S(2)}, u32[]{:S(2)}) collective-permute-start(bf16[16,512]{1,0:T(8,128)(2,1)S(1)} %get-tuple-element.209), channel_id=1, source_target_pairs={{0,3},{1,0},{2,1},{3,2},{4,7},{5,4},{6,5},{7,6},{8,11},{9,8},{10,9... | collective-permute-start | bytes 49160 | tf_op jit(solution)/shard_map/ppermute | solution.py:671
  425.9 41.1 %collective-permute-start.32 = (bf16[256,512]{1,0:T(8,128)(2,1)S(1)}, bf16[256,512]{1,0:T(8,128)(2,1)S(1)}, u32[]{:S(2)}, u32[]{:S(2)}) collective-permute-start(bf16[256,512]{1,0:T(8,128)(2,1)S(1)} %maximum_select_fusion.1), channel_id=1, source_target_pairs={{0,4},{4,0},{8,12},{12,8},{16,20},{20,16},{24,28},{28,24},{1,5},{5... | collective-permute-start | bytes 786440 | tf_op jit(solution)/shard_map/ppermute | solution.py:676
  (64 other events, 1355.9 us)
Sparse Core Ops, SparseCore 0:
  18.4 91.3 all-gather.3
  206.3 120.4 all-reduce.6
  329.8 40.1 reduce-scatter.4
  386.0 30.0 all-gather.5
